TPU v7x, 32 devices: a whole 2x2x4 slice. The times are simulated.
32 devices in a mesh: ctx: 8 (over z, x), head: 4 (over y, core).
Axes of the slice: x: 2, y: 2, z: 4, core: 2. Of those that a mesh axis runs over, the one named last changes fastest.
Arguments:
- query_in: bfloat16 [6144, 20, 128], P(('ctx', 'head')), may hold values from -24 to 24
- key_in: bfloat16 [6144, 20, 128], P(('ctx', 'head')), may hold values from -24 to 24
- value_in: bfloat16 [6144, 20, 128], P(('ctx', 'head')), may hold values from -6 to 6
- grad_out: bfloat16 [6144, 20, 128], P(('ctx', 'head')), may hold values from -6 to 6
- doc_ids: int32 [6144], replicated, may hold values from 0 to 15, never falling along the last dimension, each value on 1 to 768 neighbouring positions
- frame_kind: int32 [96], replicated, may hold values 0 or 1
Outputs:
- attn_output: bfloat16 [6144, 20, 128], P(('ctx', 'head'))
- grad_query: bfloat16 [6144, 20, 128], P(('ctx', 'head'))
- grad_key: bfloat16 [6144, 20, 128], P(('ctx', 'head'))
- grad_value: bfloat16 [6144, 20, 128], P(('ctx', 'head'))
Inputs may be any that keep to these rules, and one draw needn't show every extreme that they name: doc_ids never falls along the sequence; every document has 1 to 768 tokens and one has exactly 768.
All inputs are finite; a program needn't handle non-finite values.
Results may differ from a plain program's by a relative error of at most 0.017.
Values may be sent and summed in bfloat16 or wider, within the bound.
No kernel may reach another device: no remote copies, remote signals or barrier semaphores. Data moves between devices by JAX's collectives and lax.ppermute only.
A program may use at most 128 MiB of HBM per device.

v0:
```python
import functools
import math

import jax
import jax.numpy as jnp
from jax import lax
from jax.experimental import pallas as pl
from jax.experimental.pallas import tpu as pltpu
from jax.sharding import PartitionSpec as P

FRAME = 64
REACH = 1
AXES = ("ctx", "head")
GROUP = 4
MASKED = -1e30
CHUNKS = (2, 2, 2, 2, 2)
INFLIGHT = 2


def dot(a, b, dims):
    return lax.dot_general(a, b, (dims, ((), ())), preferred_element_type=jnp.float32)


NT = ((1,), (1,))
TN = ((0,), (0,))
NN = ((1,), (0,))


def forward_kernel(q_ref, kv0_ref, kv1_ref, kv2_ref, rows_ref, cols_ref, out_ref, stat_ref, *, scale):
    span = q_ref.shape[2]
    factor = scale * math.log2(math.e)
    cuts = (0, 256, span) if span > 256 else (0, span)
    for a, b in zip(cuts[:-1], cuts[1:]):
        query = q_ref[0, 0, a:b, :]
        grad = q_ref[1, 0, a:b, :]
        doc_row = rows_ref[0:1, a:b]
        limit_row = rows_ref[1:2, a:b]
        segments = ((kv2_ref, a, span, 0), (kv1_ref, 0, span, span), (kv0_ref, 0, b, 2 * span))
        scores = []
        for ref, lo, hi, offset in segments:
            raw = dot(ref[0, 0, lo:hi, :], query, NT) * factor
            key_doc = cols_ref[offset + lo : offset + hi, :]
            allowed = key_doc == doc_row
            if ref is kv0_ref:
                place = lo + lax.broadcasted_iota(jnp.int32, raw.shape, 0)
                allowed = allowed & (place <= limit_row)
            scores.append(jnp.where(allowed, raw, MASKED))
        top = functools.reduce(jnp.maximum, [jnp.max(s, axis=0, keepdims=True) for s in scores])
        raised = [jnp.exp2(s - top) for s in scores]
        total = functools.reduce(jnp.add, [jnp.sum(r, axis=0, keepdims=True) for r in raised])
        inverse = 1.0 / total
        probs = [r * inverse for r in raised]
        mixed = functools.reduce(
            jnp.add,
            [
                dot(ref[1, 0, lo:hi, :], p.astype(jnp.bfloat16), TN)
                for (ref, lo, hi, _), p in zip(segments, probs)
            ],
        )
        output = mixed.astype(jnp.bfloat16)
        grad_t = grad.astype(jnp.float32).T
        delta = jnp.sum(grad_t * output.astype(jnp.float32), axis=0, keepdims=True)
        grad_query = jnp.zeros_like(mixed)
        for (ref, lo, hi, _), p in zip(segments, probs):
            grad_prob = dot(ref[1, 0, lo:hi, :], grad, NT)
            grad_score = (p * (grad_prob - delta)).astype(jnp.bfloat16)
            grad_query += dot(ref[0, 0, lo:hi, :], grad_score, TN)
        out_ref[0, 0, a:b, :] = mixed.T.astype(jnp.bfloat16)
        out_ref[1, 0, a:b, :] = (grad_query * scale).T.astype(jnp.bfloat16)
        stat_ref[0, 0:1, a:b] = top + jnp.log2(total)
        stat_ref[0, 1:2, a:b] = delta


def backward_kernel(kv_ref, q0_ref, q1_ref, q2_ref, st0_ref, st1_ref, st2_ref, rows_ref, cols_ref, out_ref, *, scale):
    span = kv_ref.shape[2]
    factor = scale * math.log2(math.e)
    for a in range(0, span, 128):
        b = a + 128
        key = kv_ref[0, 0, a:b, :]
        value = kv_ref[1, 0, a:b, :]
        key_doc = cols_ref[a:b, :]
        grad_key = jnp.zeros((b - a, key.shape[1]), jnp.float32)
        grad_value = jnp.zeros((b - a, key.shape[1]), jnp.float32)
        segments = (
            (q0_ref, st0_ref, a, span, 0),
            (q1_ref, st1_ref, 0, span, span),
            (q2_ref, st2_ref, 0, b, 2 * span),
        )
        for ref, stats, lo, hi, offset in segments:
            query = ref[0, 0, lo:hi, :]
            grad = ref[1, 0, lo:hi, :]
            raw = dot(key, query, NT) * factor
            allowed = key_doc == rows_ref[0:1, offset + lo : offset + hi]
            if ref is q0_ref:
                place = a + lax.broadcasted_iota(jnp.int32, raw.shape, 0)
                allowed = allowed & (place <= rows_ref[1:2, lo:hi])
            probs = jnp.exp2(jnp.where(allowed, raw - stats[0, 0:1, lo:hi], MASKED))
            grad_value += dot(probs.astype(jnp.bfloat16), grad, NN)
            grad_prob = dot(value, grad, NT)
            grad_score = (probs * (grad_prob - stats[0, 1:2, lo:hi])).astype(jnp.bfloat16)
            grad_key += dot(grad_score, query, NN)
        out_ref[0, 0, a:b, :] = (grad_key * scale).astype(jnp.bfloat16)
        out_ref[1, 0, a:b, :] = grad_value.astype(jnp.bfloat16)


def per_head(shape):
    return pl.BlockSpec((shape[0], 1) + shape[2:], lambda h: (0, h, 0, 0))


def per_head_stats(shape):
    return pl.BlockSpec((1,) + shape[1:], lambda h: (h, 0, 0))


def whole(shape):
    return pl.BlockSpec(shape, lambda h: (0,) * len(shape))


def cost(heads, span, dim, matmuls):
    pairs = heads * span * span * 3
    return pl.CostEstimate(
        flops=2 * pairs * dim * matmuls, bytes_accessed=heads * span * dim * 2 * 10, transcendentals=pairs
    )


def attend_forward(q, kv0, kv1, kv2, rows, cols, scale):
    _, heads, span, dim = q.shape
    return pl.pallas_call(
        functools.partial(forward_kernel, scale=scale),
        grid=(heads,),
        in_specs=[per_head(q.shape)] * 4 + [whole(rows.shape), whole(cols.shape)],
        out_specs=[per_head(q.shape), per_head_stats((heads, 2, span))],
        out_shape=[
            jax.ShapeDtypeStruct(q.shape, jnp.bfloat16),
            jax.ShapeDtypeStruct((heads, 2, span), jnp.float32),
        ],
        compiler_params=pltpu.CompilerParams(vmem_limit_bytes=40 * 2**20),
        cost_estimate=cost(heads, span, dim, 4),
    )(q, kv0, kv1, kv2, rows, cols)


def attend_backward(kv, q0, q1, q2, st0, st1, st2, rows, cols, scale):
    _, heads, span, dim = kv.shape
    return pl.pallas_call(
        functools.partial(backward_kernel, scale=scale),
        grid=(heads,),
        in_specs=[per_head(kv.shape)] * 4
        + [per_head_stats(st0.shape)] * 3
        + [whole(rows.shape), whole(cols.shape)],
        out_specs=per_head(kv.shape),
        out_shape=jax.ShapeDtypeStruct(kv.shape, jnp.bfloat16),
        compiler_params=pltpu.CompilerParams(vmem_limit_bytes=40 * 2**20),
        cost_estimate=cost(heads, span, dim, 4),
    )(kv, q0, q1, q2, st0, st1, st2, rows, cols)


def tied(x, *after):
    return lax.optimization_barrier((x,) + after)[0] if after else x


def local(query_in, key_in, value_in, grad_out, doc_ids, frame_kind):
    rows_own, heads, dim = query_in.shape
    half = heads // 2
    span = 2 * rows_own
    count = lax.axis_size("ctx") * lax.axis_size("head")
    at = lax.axis_index("ctx") * lax.axis_size("head") + lax.axis_index("head")
    core = at % 2
    side = (at // 2) % 2
    base = (at - core) * rows_own
    scale = dim**-0.5

    def shifted(x, by):
        return lax.ppermute(x, AXES, [(i, i + by) for i in range(count) if 0 <= i + by < count])

    def swapped(x, bit):
        return lax.ppermute(x, AXES, [(i, i ^ bit) for i in range(count)])

    reach = 2 * span
    docs = jnp.concatenate(
        [jnp.full((reach,), -1, jnp.int32), doc_ids, jnp.full((reach,), -2, jnp.int32)]
    )
    docs = lax.dynamic_slice_in_dim(docs, base, 5 * span)
    kinds = jnp.concatenate([frame_kind, jnp.zeros((reach // FRAME,), jnp.int32)])
    kinds = lax.dynamic_slice_in_dim(kinds, base // FRAME, 3 * span // FRAME)
    place = jnp.arange(3 * span, dtype=jnp.int32)
    limit = jnp.where(jnp.repeat(kinds, FRAME) == 1, (place // FRAME) * FRAME + FRAME - 1, place)
    rows = jnp.stack([docs[reach:], limit])
    cols = docs[: 3 * span, None]

    def halves(x, y, which):
        pick = lambda a: lax.dynamic_slice_in_dim(a.transpose(1, 0, 2), which * half, half, 0)
        return jnp.stack([pick(x), pick(y)])

    def pieces(x, y):
        own = halves(x, y, core)
        came = swapped(halves(x, y, 1 - core), 1)
        out, start = [], 0
        for size in CHUNKS:
            a, b = own[:, start : start + size], came[:, start : start + size]
            first, second = jnp.where(core == 0, a, b), jnp.where(core == 0, b, a)
            out.append(jnp.concatenate([first, second], axis=2))
            start += size
        return out

    kv0 = pieces(key_in, value_in)
    q0 = pieces(query_in, grad_out)
    n = len(CHUNKS)
    far, near = [], []
    for j in range(2 * n):
        mine = kv0[j] if j < n else q0[j - n]
        after = [far[j - INFLIGHT]] if j >= INFLIGHT else []
        far.append(shifted(tied(mine, *after), GROUP if j < n else -GROUP))
    for j in range(2 * n):
        if j < n:
            sent = jnp.where(side == 0, kv0[j], far[j])
        else:
            sent = jnp.where(side == 0, far[j], q0[j - n])
        after = [near[j - INFLIGHT]] if j >= INFLIGHT else []
        near.append(swapped(tied(sent, *after), 2))

    forward = [
        attend_forward(q0[j], kv0[j], near[j], far[j], rows[:, :span], cols, scale) for j in range(n)
    ]
    st0 = jnp.concatenate([f[1] for f in forward], axis=0)
    st2 = shifted(st0, -GROUP)
    st1 = swapped(jnp.where(side == 0, st2, st0), 2)
    own_cols = cols[2 * span :]
    outs, start = [], 0
    for j, size in enumerate(CHUNKS):
        cut = slice(start, start + size)
        outs.append(
            attend_backward(
                kv0[j], q0[j], near[n + j], far[n + j], st0[cut], st1[cut], st2[cut], rows, own_cols, scale
            )
        )
        start += size

    def returned(parts):
        keep, back = [], []
        for part in parts:
            low, high = part[:, :, :rows_own], part[:, :, rows_own:]
            keep.append(jnp.where(core == 0, low, high))
            back.append(swapped(jnp.where(core == 0, high, low), 1))
        keep = jnp.concatenate(keep, axis=1)
        back = jnp.concatenate(back, axis=1)
        both = jnp.concatenate([jnp.where(core == 0, keep, back), jnp.where(core == 0, back, keep)], axis=1)
        return both[0].transpose(1, 0, 2), both[1].transpose(1, 0, 2)

    output, grad_query = returned([jnp.concatenate([f[0] for f in forward], axis=1)])
    grad_key, grad_value = returned(outs)
    return output, grad_query, grad_key, grad_value


def solution(mesh):
    placed = P(AXES, None, None)
    return jax.shard_map(
        local,
        mesh=mesh,
        in_specs=(placed,) * 4 + (P(), P()),
        out_specs=(placed,) * 4,
        check_vma=False,
    )
```

profile of v0, /device:TPU:27, one launch (start us, length us, event | category | flops | bytes accessed | tf_op | source)
XLA Modules:
  0.0 158.1 jit_solution(757312580490340970)
XLA Ops:
  0.7 1.6 %dynamic-slice_bitcast_fusion.2 = (bf16[1,10,192,128]{3,2,1,0:T(8,128)(2,1)S(1)}, bf16[1,10,192,128]{3,2,1,0:T(8,128)(2,1)S(1)}, bf16[1,10,192,128]{3,2,1,0:T(8,128)(2,1)S(1)}, bf16[1,10,192,128]{3,2,1,0:T(8,128)(2,1)S(1)}) fusion(bf16[192,20,128]{2,0,1:T(8,128)(2,1)} %param.8, s32[]{:T(128)S(6)} %select_n.265, s32[]{:T(128)S(6)} %select_n.266, ...), kind=kLoop, calls=%fused_computation.38 | loop fusion | bytes 3932168 | tf_op jit(solution)/shard_map/stack | solution.py:191
  6.9 1.3 broadcast_select_fusion.22
  12.5 8.3 %collective-permute-done.4.kv2_ref = bf16[2,2,384,128]{3,2,1,0:T(8,128)(2,1)S(1)} collective-permute-done((bf16[2,2,384,128]{3,2,1,0:T(8,128)(2,1)S(1)}, bf16[2,2,384,128]{3,2,1,0:T(8,128)(2,1)S(1)}, u32[]{:S(2)}, u32[]{:S(2)}) %collective-permute-start.4) | collective-permute-done | bytes 393248 | tf_op jit(solution)/shard_map/ppermute | solution.py:172
  22.2 1.3 collective-permute-start.5
  23.5 5.7 %collective-permute-done.2.kv2_ref = bf16[2,2,384,128]{3,2,1,0:T(8,128)(2,1)S(1)} collective-permute-done((bf16[2,2,384,128]{3,2,1,0:T(8,128)(2,1)S(1)}, bf16[2,2,384,128]{3,2,1,0:T(8,128)(2,1)S(1)}, u32[]{:S(2)}, u32[]{:S(2)}) %collective-permute-start.2) | collective-permute-done | bytes 393248 | tf_op jit(solution)/shard_map/ppermute | solution.py:172
  29.3 1.3 collective-permute-start.3
  32.0 5.6 %collective-permute-done.8.kv2_ref = bf16[2,2,384,128]{3,2,1,0:T(8,128)(2,1)S(1)} collective-permute-done((bf16[2,2,384,128]{3,2,1,0:T(8,128)(2,1)S(1)}, bf16[2,2,384,128]{3,2,1,0:T(8,128)(2,1)S(1)}, u32[]{:S(2)}, u32[]{:S(2)}) %collective-permute-start.8) | collective-permute-done | bytes 393248 | tf_op jit(solution)/shard_map/ppermute | solution.py:172
  37.7 3.1 %collective-permute-start.13 = (bf16[2,2,384,128]{3,2,1,0:T(8,128)(2,1)S(1)}, bf16[2,2,384,128]{3,2,1,0:T(8,128)(2,1)S(1)}, u32[]{:S(2)}, u32[]{:S(2)}) collective-permute-start(bf16[2,2,384,128]{3,2,1,0:T(8,128)(2,1)S(1)} %pad_maximum_fusion.4.q_ref.q0_ref), channel_id=1, source_target_pairs={{4,0},{5,1},{6,2},{7,3},{8,4},{9,5},{10,6},{11,7},{12,8},{13,9},{1... | collective-permute-start | bytes 1179656 | tf_op jit(solution)/shard_map/ppermute | solution.py:172
  42.2 4.4 %shard_map.93 = (bf16[2,2,384,128]{3,2,1,0:T(8,128)(2,1)S(1)}, f32[2,2,384]{2,1,0:T(2,128)S(1)}) custom-call(bf16[2,2,384,128]{3,2,1,0:T(8,128)(2,1)S(1)} %pad_maximum_fusion.4.q_ref.q0_ref, bf16[2,2,384,128]{3,2,1,0:T(8,128)(2,1)S(1)} %pad_maximum_fusion.5.kv0_ref.kv_ref, bf16[2,2,384,128]{3,2,1,0:T(8,128)(2,1)S(1)} %collective-permute-done.3.kv1_ref, ...), custom_call_target="tpu_custom_call" | custom-call | flops 905969664 | bytes 1966080 | tf_op jit(solution)/shard_map/pallas_call | solution.py:127
  48.8 4.4 %shard_map.94 = (bf16[2,2,384,128]{3,2,1,0:T(8,128)(2,1)S(1)}, f32[2,2,384]{2,1,0:T(2,128)S(1)}) custom-call(bf16[2,2,384,128]{3,2,1,0:T(8,128)(2,1)S(1)} %pad_maximum_fusion.6.q_ref.q0_ref, bf16[2,2,384,128]{3,2,1,0:T(8,128)(2,1)S(1)} %pad_maximum_fusion.7.kv0_ref.kv_ref, bf16[2,2,384,128]{3,2,1,0:T(8,128)(2,1)S(1)} %collective-permute-done.5.kv1_ref, ...), custom_call_target="tpu_custom_call" | custom-call | flops 905969664 | bytes 1966080 | tf_op jit(solution)/shard_map/pallas_call | solution.py:127
  53.8 4.1 %collective-permute-start.19 = (bf16[2,2,384,128]{3,2,1,0:T(8,128)(2,1)S(1)}, bf16[2,2,384,128]{3,2,1,0:T(8,128)(2,1)S(1)}, u32[]{:S(2)}, u32[]{:S(2)}) collective-permute-start(bf16[2,2,384,128]{3,2,1,0:T(8,128)(2,1)S(1)} %pad_maximum_fusion.8.q_ref.q0_ref), channel_id=1, source_target_pairs={{4,0},{5,1},{6,2},{7,3},{8,4},{9,5},{10,6},{11,7},{12,8},{13,9},{1... | collective-permute-start | bytes 1179656 | tf_op jit(solution)/shard_map/ppermute | solution.py:172
  58.1 1.3 collective-permute-start.14
  59.8 10.0 %collective-permute-start.17 = (bf16[2,2,384,128]{3,2,1,0:T(8,128)(2,1)S(1)}, bf16[2,2,384,128]{3,2,1,0:T(8,128)(2,1)S(1)}, u32[]{:S(2)}, u32[]{:S(2)}) collective-permute-start(bf16[2,2,384,128]{3,2,1,0:T(8,128)(2,1)S(1)} %pad_maximum_fusion.6.q_ref.q0_ref), channel_id=1, source_target_pairs={{4,0},{5,1},{6,2},{7,3},{8,4},{9,5},{10,6},{11,7},{12,8},{13,9},{1... | collective-permute-start | bytes 1179656 | tf_op jit(solution)/shard_map/ppermute | solution.py:172
  69.9 4.4 %shard_map.95 = (bf16[2,2,384,128]{3,2,1,0:T(8,128)(2,1)S(1)}, f32[2,2,384]{2,1,0:T(2,128)S(1)}) custom-call(bf16[2,2,384,128]{3,2,1,0:T(8,128)(2,1)S(1)} %pad_maximum_fusion.8.q_ref.q0_ref, bf16[2,2,384,128]{3,2,1,0:T(8,128)(2,1)S(1)} %pad_maximum_fusion.9.kv0_ref.kv_ref, bf16[2,2,384,128]{3,2,1,0:T(8,128)(2,1)S(1)} %collective-permute-done.7.kv1_ref, ...), custom_call_target="tpu_custom_call" | custom-call | flops 905969664 | bytes 1966080 | tf_op jit(solution)/shard_map/pallas_call | solution.py:127
  74.3 4.4 %shard_map.96 = (bf16[2,2,384,128]{3,2,1,0:T(8,128)(2,1)S(1)}, f32[2,2,384]{2,1,0:T(2,128)S(1)}) custom-call(bf16[2,2,384,128]{3,2,1,0:T(8,128)(2,1)S(1)} %pad_maximum_fusion.10.q_ref.q0_ref, bf16[2,2,384,128]{3,2,1,0:T(8,128)(2,1)S(1)} %pad_maximum_fusion.11.kv0_ref.kv_ref, bf16[2,2,384,128]{3,2,1,0:T(8,128)(2,1)S(1)} %collective-permute-done.9.kv1_ref, ...), custom_call_target="tpu_custom_call" | custom-call | flops 905969664 | bytes 1966080 | tf_op jit(solution)/shard_map/pallas_call | solution.py:127
  78.8 3.2 %collective-permute-start.23 = (bf16[2,2,384,128]{3,2,1,0:T(8,128)(2,1)S(1)}, bf16[2,2,384,128]{3,2,1,0:T(8,128)(2,1)S(1)}, u32[]{:S(2)}, u32[]{:S(2)}) collective-permute-start(bf16[2,2,384,128]{3,2,1,0:T(8,128)(2,1)S(1)} %pad_maximum_fusion.12.q_ref.q0_ref), channel_id=1, source_target_pairs={{4,0},{5,1},{6,2},{7,3},{8,4},{9,5},{10,6},{11,7},{12,8},{13,9},{1... | collective-permute-start | bytes 1179656 | tf_op jit(solution)/shard_map/ppermute | solution.py:172
  83.5 4.4 %shard_map.97 = (bf16[2,2,384,128]{3,2,1,0:T(8,128)(2,1)S(1)}, f32[2,2,384]{2,1,0:T(2,128)S(1)}) custom-call(bf16[2,2,384,128]{3,2,1,0:T(8,128)(2,1)S(1)} %pad_maximum_fusion.12.q_ref.q0_ref, bf16[2,2,384,128]{3,2,1,0:T(8,128)(2,1)S(1)} %pad_maximum_fusion.13.kv0_ref.kv_ref, bf16[2,2,384,128]{3,2,1,0:T(8,128)(2,1)S(1)} %collective-permute-done.11.kv1_ref, ...), custom_call_target="tpu_custom_call" | custom-call | flops 905969664 | bytes 1966080 | tf_op jit(solution)/shard_map/pallas_call | solution.py:127
  87.9 2.1 %collective-permute-start.15 = (f32[10,2,384]{2,1,0:T(2,128)S(1)}, f32[10,2,384]{2,1,0:T(2,128)S(1)}, u32[]{:S(2)}, u32[]{:S(2)}) collective-permute-start(f32[10,2,384]{2,1,0:T(2,128)S(1)} %constant_dynamic-update-slice_fusion.5), channel_id=1, source_target_pairs={{4,0},{5,1},{6,2},{7,3},{8,4},{9,5},{10,6},{11,7},{12,8},{13,9},{1... | collective-permute-start | bytes 92168 | tf_op jit(solution)/shard_map/ppermute | solution.py:172
  90.0 3.1 %collective-permute-start.21 = (bf16[2,2,384,128]{3,2,1,0:T(8,128)(2,1)S(1)}, bf16[2,2,384,128]{3,2,1,0:T(8,128)(2,1)S(1)}, u32[]{:S(2)}, u32[]{:S(2)}) collective-permute-start(bf16[2,2,384,128]{3,2,1,0:T(8,128)(2,1)S(1)} %pad_maximum_fusion.10.q_ref.q0_ref), channel_id=1, source_target_pairs={{4,0},{5,1},{6,2},{7,3},{8,4},{9,5},{10,6},{11,7},{12,8},{13,9},{1... | collective-permute-start | bytes 1179656 | tf_op jit(solution)/shard_map/ppermute | solution.py:172
  93.6 1.3 collective-permute-start.16
  94.9 5.3 %collective-permute-done.16 = f32[10,2,384]{2,1,0:T(2,128)S(1)} collective-permute-done((f32[10,2,384]{2,1,0:T(2,128)S(1)}, f32[10,2,384]{2,1,0:T(2,128)S(1)}, u32[]{:S(2)}, u32[]{:S(2)}) %collective-permute-start.16) | collective-permute-done | bytes 30752 | tf_op jit(solution)/shard_map/ppermute | solution.py:175
  100.2 4.5 %shard_map.98 = bf16[2,2,384,128]{3,2,1,0:T(8,128)(2,1)S(1)} custom-call(bf16[2,2,384,128]{3,2,1,0:T(8,128)(2,1)S(1)} %pad_maximum_fusion.5.kv0_ref.kv_ref, bf16[2,2,384,128]{3,2,1,0:T(8,128)(2,1)S(1)} %pad_maximum_fusion.4.q_ref.q0_ref, bf16[2,2,384,128]{3,2,1,0:T(8,128)(2,1)S(1)} %collective-permute-done.14.q1_ref, ...), custom_call_target="tpu_custom_call" | custom-call | flops 905969664 | bytes 1966080 | tf_op jit(solution)/shard_map/pallas_call | solution.py:143
  104.8 17.6 %collective-permute-start.25 = (bf16[2,2,192,128]{3,2,1,0:T(8,128)(2,1)S(1)}, bf16[2,2,192,128]{3,2,1,0:T(8,128)(2,1)S(1)}, u32[]{:S(2)}, u32[]{:S(2)}) collective-permute-start(bf16[2,2,192,128]{3,2,1,0:T(8,128)(2,1)S(1)} %get-tuple-element.102), channel_id=1, source_target_pairs={{0,1},{1,0},{2,3},{3,2},{4,5},{5,4},{6,7},{7,6},{8,9},{9,8},{10,11... | collective-permute-start | bytes 589832 | tf_op jit(solution)/shard_map/ppermute | solution.py:175
  124.4 1.3 collective-permute-start.22
  125.7 4.5 %shard_map.99 = bf16[2,2,384,128]{3,2,1,0:T(8,128)(2,1)S(1)} custom-call(bf16[2,2,384,128]{3,2,1,0:T(8,128)(2,1)S(1)} %pad_maximum_fusion.7.kv0_ref.kv_ref, bf16[2,2,384,128]{3,2,1,0:T(8,128)(2,1)S(1)} %pad_maximum_fusion.6.q_ref.q0_ref, bf16[2,2,384,128]{3,2,1,0:T(8,128)(2,1)S(1)} %collective-permute-done.18.q1_ref, ...), custom_call_target="tpu_custom_call" | custom-call | flops 905969664 | bytes 1966080 | tf_op jit(solution)/shard_map/pallas_call | solution.py:143
  131.1 4.5 %shard_map.100 = bf16[2,2,384,128]{3,2,1,0:T(8,128)(2,1)S(1)} custom-call(bf16[2,2,384,128]{3,2,1,0:T(8,128)(2,1)S(1)} %pad_maximum_fusion.9.kv0_ref.kv_ref, bf16[2,2,384,128]{3,2,1,0:T(8,128)(2,1)S(1)} %pad_maximum_fusion.8.q_ref.q0_ref, bf16[2,2,384,128]{3,2,1,0:T(8,128)(2,1)S(1)} %collective-permute-done.20.q1_ref, ...), custom_call_target="tpu_custom_call" | custom-call | flops 905969664 | bytes 1966080 | tf_op jit(solution)/shard_map/pallas_call | solution.py:143
  135.8 7.3 %collective-permute-done.22.q1_ref = bf16[2,2,384,128]{3,2,1,0:T(8,128)(2,1)S(1)} collective-permute-done((bf16[2,2,384,128]{3,2,1,0:T(8,128)(2,1)S(1)}, bf16[2,2,384,128]{3,2,1,0:T(8,128)(2,1)S(1)}, u32[]{:S(2)}, u32[]{:S(2)}) %collective-permute-start.22) | collective-permute-done | bytes 393248 | tf_op jit(solution)/shard_map/ppermute | solution.py:175
  143.1 4.5 %shard_map.101 = bf16[2,2,384,128]{3,2,1,0:T(8,128)(2,1)S(1)} custom-call(bf16[2,2,384,128]{3,2,1,0:T(8,128)(2,1)S(1)} %pad_maximum_fusion.11.kv0_ref.kv_ref, bf16[2,2,384,128]{3,2,1,0:T(8,128)(2,1)S(1)} %pad_maximum_fusion.10.q_ref.q0_ref, bf16[2,2,384,128]{3,2,1,0:T(8,128)(2,1)S(1)} %collective-permute-done.22.q1_ref, ...), custom_call_target="tpu_custom_call" | custom-call | flops 905969664 | bytes 1966080 | tf_op jit(solution)/shard_map/pallas_call | solution.py:143
  148.7 4.5 %shard_map.102 = bf16[2,2,384,128]{3,2,1,0:T(8,128)(2,1)S(1)} custom-call(bf16[2,2,384,128]{3,2,1,0:T(8,128)(2,1)S(1)} %pad_maximum_fusion.13.kv0_ref.kv_ref, bf16[2,2,384,128]{3,2,1,0:T(8,128)(2,1)S(1)} %pad_maximum_fusion.12.q_ref.q0_ref, bf16[2,2,384,128]{3,2,1,0:T(8,128)(2,1)S(1)} %collective-permute-done.24.q1_ref, ...), custom_call_target="tpu_custom_call" | custom-call | flops 905969664 | bytes 1966080 | tf_op jit(solution)/shard_map/pallas_call | solution.py:143
  153.5 1.3 collective-permute-done.29
  155.0 1.4 fusion.4
  156.6 1.4 fusion.5
  (116 shorter events, 23.1 us)
Async XLA Ops:
  2.3 1.8 %copy-start.1 = (bf16[192,20,128]{2,0,1:T(8,128)(2,1)S(1)}, bf16[192,20,128]{2,0,1:T(8,128)(2,1)}, u32[]{:S(2)}) copy-start(bf16[192,20,128]{2,0,1:T(8,128)(2,1)} %param.6) | copy-start | bytes 2949124
  3.4 3.5 %collective-permute-start.1 = (bf16[2,10,192,128]{3,2,1,0:T(8,128)(2,1)}, bf16[2,10,192,128]{3,2,1,0:T(8,128)(2,1)}, u32[]{:S(2)}, u32[]{:S(2)}) collective-permute-start(bf16[2,10,192,128]{3,2,1,0:T(8,128)(2,1)} %pad_maximum_fusion.3), channel_id=1, source_target_pairs={{0,1},{1,0},{2,3},{3,2},{4,5},{5,4},{6,7},{7,6},{8,9},{9,8},{10,11... | collective-permute-start | bytes 2949128 | tf_op jit(solution)/shard_map/ppermute | solution.py:175
  4.3 2.0 %copy-start.2 = (s32[6144]{0:T(1024)S(1)}, s32[6144]{0:T(1024)}, u32[]{:S(2)}) copy-start(s32[6144]{0:T(1024)} %param.10) | copy-start | bytes 73732
  5.4 6.7 %collective-permute-start = (bf16[2,10,192,128]{3,2,1,0:T(8,128)(2,1)}, bf16[2,10,192,128]{3,2,1,0:T(8,128)(2,1)S(1)}, u32[]{:S(2)}, u32[]{:S(2)}) collective-permute-start(bf16[2,10,192,128]{3,2,1,0:T(8,128)(2,1)} %pad_maximum_fusion.2), channel_id=1, source_target_pairs={{0,1},{1,0},{2,3},{3,2},{4,5},{5,4},{6,7},{7,6},{8,9},{9,8},{10,11... | collective-permute-start | bytes 2949128 | tf_op jit(solution)/shard_map/ppermute | solution.py:175
  8.2 12.6 %collective-permute-start.4 = (bf16[2,2,384,128]{3,2,1,0:T(8,128)(2,1)S(1)}, bf16[2,2,384,128]{3,2,1,0:T(8,128)(2,1)S(1)}, u32[]{:S(2)}, u32[]{:S(2)}) collective-permute-start(bf16[2,2,384,128]{3,2,1,0:T(8,128)(2,1)S(1)} %pad_maximum_fusion.7.kv0_ref.kv_ref), channel_id=1, source_target_pairs={{0,4},{1,5},{2,6},{3,7},{4,8},{5,9},{6,10},{7,11},{8,12},{9,13},{1... | collective-permute-start | bytes 1179656 | tf_op jit(solution)/shard_map/ppermute | solution.py:172
  9.6 19.7 %collective-permute-start.2 = (bf16[2,2,384,128]{3,2,1,0:T(8,128)(2,1)S(1)}, bf16[2,2,384,128]{3,2,1,0:T(8,128)(2,1)S(1)}, u32[]{:S(2)}, u32[]{:S(2)}) collective-permute-start(bf16[2,2,384,128]{3,2,1,0:T(8,128)(2,1)S(1)} %pad_maximum_fusion.5.kv0_ref.kv_ref), channel_id=1, source_target_pairs={{0,4},{1,5},{2,6},{3,7},{4,8},{5,9},{6,10},{7,11},{8,12},{9,13},{1... | collective-permute-start | bytes 1179656 | tf_op jit(solution)/shard_map/ppermute | solution.py:172
  20.8 16.9 %collective-permute-start.8 = (bf16[2,2,384,128]{3,2,1,0:T(8,128)(2,1)S(1)}, bf16[2,2,384,128]{3,2,1,0:T(8,128)(2,1)S(1)}, u32[]{:S(2)}, u32[]{:S(2)}) collective-permute-start(bf16[2,2,384,128]{3,2,1,0:T(8,128)(2,1)S(1)} %pad_maximum_fusion.11.kv0_ref.kv_ref), channel_id=1, source_target_pairs={{0,4},{1,5},{2,6},{3,7},{4,8},{5,9},{6,10},{7,11},{8,12},{9,13},{1... | collective-permute-start | bytes 1179656 | tf_op jit(solution)/shard_map/ppermute | solution.py:172
  22.2 18.6 %collective-permute-start.5 = (bf16[2,2,384,128]{3,2,1,0:T(8,128)(2,1)S(1)}, bf16[2,2,384,128]{3,2,1,0:T(8,128)(2,1)S(1)}, u32[]{:S(2)}, u32[]{:S(2)}) collective-permute-start(bf16[2,2,384,128]{3,2,1,0:T(8,128)(2,1)S(1)} %broadcast_select_fusion.14), channel_id=1, source_target_pairs={{0,2},{1,3},{2,0},{3,1},{4,6},{5,7},{6,4},{7,5},{8,10},{9,11},{10,... | collective-permute-start | bytes 1179656 | tf_op jit(solution)/shard_map/ppermute | solution.py:175
  29.3 12.8 %collective-permute-start.3 = (bf16[2,2,384,128]{3,2,1,0:T(8,128)(2,1)S(1)}, bf16[2,2,384,128]{3,2,1,0:T(8,128)(2,1)S(1)}, u32[]{:S(2)}, u32[]{:S(2)}) collective-permute-start(bf16[2,2,384,128]{3,2,1,0:T(8,128)(2,1)S(1)} %broadcast_select_fusion.15), channel_id=1, source_target_pairs={{0,2},{1,3},{2,0},{3,1},{4,6},{5,7},{6,4},{7,5},{8,10},{9,11},{10,... | collective-permute-start | bytes 1179656 | tf_op jit(solution)/shard_map/ppermute | solution.py:175
  30.7 15.9 %collective-permute-start.6 = (bf16[2,2,384,128]{3,2,1,0:T(8,128)(2,1)S(1)}, bf16[2,2,384,128]{3,2,1,0:T(8,128)(2,1)S(1)}, u32[]{:S(2)}, u32[]{:S(2)}) collective-permute-start(bf16[2,2,384,128]{3,2,1,0:T(8,128)(2,1)S(1)} %pad_maximum_fusion.9.kv0_ref.kv_ref), channel_id=1, source_target_pairs={{0,4},{1,5},{2,6},{3,7},{4,8},{5,9},{6,10},{7,11},{8,12},{9,13},{1... | collective-permute-start | bytes 1179656 | tf_op jit(solution)/shard_map/ppermute | solution.py:172
  37.7 16.2 %collective-permute-start.13 = (bf16[2,2,384,128]{3,2,1,0:T(8,128)(2,1)S(1)}, bf16[2,2,384,128]{3,2,1,0:T(8,128)(2,1)S(1)}, u32[]{:S(2)}, u32[]{:S(2)}) collective-permute-start(bf16[2,2,384,128]{3,2,1,0:T(8,128)(2,1)S(1)} %pad_maximum_fusion.4.q_ref.q0_ref), channel_id=1, source_target_pairs={{4,0},{5,1},{6,2},{7,3},{8,4},{9,5},{10,6},{11,7},{12,8},{13,9},{1... | collective-permute-start | bytes 1179656 | tf_op jit(solution)/shard_map/ppermute | solution.py:172
  40.9 17.2 %collective-permute-start.9 = (bf16[2,2,384,128]{3,2,1,0:T(8,128)(2,1)S(1)}, bf16[2,2,384,128]{3,2,1,0:T(8,128)(2,1)S(1)}, u32[]{:S(2)}, u32[]{:S(2)}) collective-permute-start(bf16[2,2,384,128]{3,2,1,0:T(8,128)(2,1)S(1)} %broadcast_select_fusion.12), channel_id=1, source_target_pairs={{0,2},{1,3},{2,0},{3,1},{4,6},{5,7},{6,4},{7,5},{8,10},{9,11},{10,... | collective-permute-start | bytes 1179656 | tf_op jit(solution)/shard_map/ppermute | solution.py:175
  46.7 12.8 %collective-permute-start.7 = (bf16[2,2,384,128]{3,2,1,0:T(8,128)(2,1)S(1)}, bf16[2,2,384,128]{3,2,1,0:T(8,128)(2,1)S(1)}, u32[]{:S(2)}, u32[]{:S(2)}) collective-permute-start(bf16[2,2,384,128]{3,2,1,0:T(8,128)(2,1)S(1)} %broadcast_select_fusion.13), channel_id=1, source_target_pairs={{0,2},{1,3},{2,0},{3,1},{4,6},{5,7},{6,4},{7,5},{8,10},{9,11},{10,... | collective-permute-start | bytes 1179656 | tf_op jit(solution)/shard_map/ppermute | solution.py:175
  47.5 11.9 %collective-permute-start.10 = (bf16[2,2,384,128]{3,2,1,0:T(8,128)(2,1)S(1)}, bf16[2,2,384,128]{3,2,1,0:T(8,128)(2,1)S(1)}, u32[]{:S(2)}, u32[]{:S(2)}) collective-permute-start(bf16[2,2,384,128]{3,2,1,0:T(8,128)(2,1)S(1)} %pad_maximum_fusion.13.kv0_ref.kv_ref), channel_id=1, source_target_pairs={{0,4},{1,5},{2,6},{3,7},{4,8},{5,9},{6,10},{7,11},{8,12},{9,13},{1... | collective-permute-start | bytes 1179656 | tf_op jit(solution)/shard_map/ppermute | solution.py:172
  53.8 25.0 %collective-permute-start.19 = (bf16[2,2,384,128]{3,2,1,0:T(8,128)(2,1)S(1)}, bf16[2,2,384,128]{3,2,1,0:T(8,128)(2,1)S(1)}, u32[]{:S(2)}, u32[]{:S(2)}) collective-permute-start(bf16[2,2,384,128]{3,2,1,0:T(8,128)(2,1)S(1)} %pad_maximum_fusion.8.q_ref.q0_ref), channel_id=1, source_target_pairs={{4,0},{5,1},{6,2},{7,3},{8,4},{9,5},{10,6},{11,7},{12,8},{13,9},{1... | collective-permute-start | bytes 1179656 | tf_op jit(solution)/shard_map/ppermute | solution.py:172
  58.1 24.1 %collective-permute-start.14 = (bf16[2,2,384,128]{3,2,1,0:T(8,128)(2,1)S(1)}, bf16[2,2,384,128]{3,2,1,0:T(8,128)(2,1)S(1)}, u32[]{:S(2)}, u32[]{:S(2)}) collective-permute-start(bf16[2,2,384,128]{3,2,1,0:T(8,128)(2,1)S(1)} %broadcast_select_fusion.10), channel_id=1, source_target_pairs={{0,2},{1,3},{2,0},{3,1},{4,6},{5,7},{6,4},{7,5},{8,10},{9,11},{10,... | collective-permute-start | bytes 1179656 | tf_op jit(solution)/shard_map/ppermute | solution.py:175
  59.5 24.0 %collective-permute-start.11 = (bf16[2,2,384,128]{3,2,1,0:T(8,128)(2,1)S(1)}, bf16[2,2,384,128]{3,2,1,0:T(8,128)(2,1)S(1)}, u32[]{:S(2)}, u32[]{:S(2)}) collective-permute-start(bf16[2,2,384,128]{3,2,1,0:T(8,128)(2,1)S(1)} %broadcast_select_fusion.11), channel_id=1, source_target_pairs={{0,2},{1,3},{2,0},{3,1},{4,6},{5,7},{6,4},{7,5},{8,10},{9,11},{10,... | collective-permute-start | bytes 1179656 | tf_op jit(solution)/shard_map/ppermute | solution.py:175
  59.8 30.1 %collective-permute-start.17 = (bf16[2,2,384,128]{3,2,1,0:T(8,128)(2,1)S(1)}, bf16[2,2,384,128]{3,2,1,0:T(8,128)(2,1)S(1)}, u32[]{:S(2)}, u32[]{:S(2)}) collective-permute-start(bf16[2,2,384,128]{3,2,1,0:T(8,128)(2,1)S(1)} %pad_maximum_fusion.6.q_ref.q0_ref), channel_id=1, source_target_pairs={{4,0},{5,1},{6,2},{7,3},{8,4},{9,5},{10,6},{11,7},{12,8},{13,9},{1... | collective-permute-start | bytes 1179656 | tf_op jit(solution)/shard_map/ppermute | solution.py:172
  78.8 45.0 %collective-permute-start.23 = (bf16[2,2,384,128]{3,2,1,0:T(8,128)(2,1)S(1)}, bf16[2,2,384,128]{3,2,1,0:T(8,128)(2,1)S(1)}, u32[]{:S(2)}, u32[]{:S(2)}) collective-permute-start(bf16[2,2,384,128]{3,2,1,0:T(8,128)(2,1)S(1)} %pad_maximum_fusion.12.q_ref.q0_ref), channel_id=1, source_target_pairs={{4,0},{5,1},{6,2},{7,3},{8,4},{9,5},{10,6},{11,7},{12,8},{13,9},{1... | collective-permute-start | bytes 1179656 | tf_op jit(solution)/shard_map/ppermute | solution.py:172
  82.2 41.8 %collective-permute-start.20 = (bf16[2,2,384,128]{3,2,1,0:T(8,128)(2,1)S(1)}, bf16[2,2,384,128]{3,2,1,0:T(8,128)(2,1)S(1)}, u32[]{:S(2)}, u32[]{:S(2)}) collective-permute-start(bf16[2,2,384,128]{3,2,1,0:T(8,128)(2,1)S(1)} %broadcast_select_fusion.8), channel_id=1, source_target_pairs={{0,2},{1,3},{2,0},{3,1},{4,6},{5,7},{6,4},{7,5},{8,10},{9,11},{10,... | collective-permute-start | bytes 1179656 | tf_op jit(solution)/shard_map/ppermute | solution.py:175
  87.9 5.7 %collective-permute-start.15 = (f32[10,2,384]{2,1,0:T(2,128)S(1)}, f32[10,2,384]{2,1,0:T(2,128)S(1)}, u32[]{:S(2)}, u32[]{:S(2)}) collective-permute-start(f32[10,2,384]{2,1,0:T(2,128)S(1)} %constant_dynamic-update-slice_fusion.5), channel_id=1, source_target_pairs={{4,0},{5,1},{6,2},{7,3},{8,4},{9,5},{10,6},{11,7},{12,8},{13,9},{1... | collective-permute-start | bytes 92168 | tf_op jit(solution)/shard_map/ppermute | solution.py:172
  90.0 34.3 %collective-permute-start.21 = (bf16[2,2,384,128]{3,2,1,0:T(8,128)(2,1)S(1)}, bf16[2,2,384,128]{3,2,1,0:T(8,128)(2,1)S(1)}, u32[]{:S(2)}, u32[]{:S(2)}) collective-permute-start(bf16[2,2,384,128]{3,2,1,0:T(8,128)(2,1)S(1)} %pad_maximum_fusion.10.q_ref.q0_ref), channel_id=1, source_target_pairs={{4,0},{5,1},{6,2},{7,3},{8,4},{9,5},{10,6},{11,7},{12,8},{13,9},{1... | collective-permute-start | bytes 1179656 | tf_op jit(solution)/shard_map/ppermute | solution.py:172
  93.2 31.2 %collective-permute-start.18 = (bf16[2,2,384,128]{3,2,1,0:T(8,128)(2,1)S(1)}, bf16[2,2,384,128]{3,2,1,0:T(8,128)(2,1)S(1)}, u32[]{:S(2)}, u32[]{:S(2)}) collective-permute-start(bf16[2,2,384,128]{3,2,1,0:T(8,128)(2,1)S(1)} %broadcast_select_fusion.9), channel_id=1, source_target_pairs={{0,2},{1,3},{2,0},{3,1},{4,6},{5,7},{6,4},{7,5},{8,10},{9,11},{10,... | collective-permute-start | bytes 1179656 | tf_op jit(solution)/shard_map/ppermute | solution.py:175
  93.6 6.6 %collective-permute-start.16 = (f32[10,2,384]{2,1,0:T(2,128)S(1)}, f32[10,2,384]{2,1,0:T(2,128)S(1)}, u32[]{:S(2)}, u32[]{:S(2)}) collective-permute-start(f32[10,2,384]{2,1,0:T(2,128)S(1)} %broadcast_select_fusion.41), channel_id=1, source_target_pairs={{0,2},{1,3},{2,0},{3,1},{4,6},{5,7},{6,4},{7,5},{8,10},{9,11},{10,... | collective-permute-start | bytes 92168 | tf_op jit(solution)/shard_map/ppermute | solution.py:175
  104.8 18.7 %collective-permute-start.25 = (bf16[2,2,192,128]{3,2,1,0:T(8,128)(2,1)S(1)}, bf16[2,2,192,128]{3,2,1,0:T(8,128)(2,1)S(1)}, u32[]{:S(2)}, u32[]{:S(2)}) collective-permute-start(bf16[2,2,192,128]{3,2,1,0:T(8,128)(2,1)S(1)} %get-tuple-element.102), channel_id=1, source_target_pairs={{0,1},{1,0},{2,3},{3,2},{4,5},{5,4},{6,7},{7,6},{8,9},{9,8},{10,11... | collective-permute-start | bytes 589832 | tf_op jit(solution)/shard_map/ppermute | solution.py:175
  123.5 33.0 %collective-permute-start.12 = (bf16[2,10,192,128]{3,2,1,0:T(8,128)(2,1)S(1)}, bf16[2,10,192,128]{3,2,1,0:T(8,128)(2,1)S(1)}, u32[]{:S(2)}, u32[]{:S(2)}) collective-permute-start(bf16[2,10,192,128]{3,2,1,0:T(8,128)(2,1)S(1)} %broadcast_select_fusion.4), channel_id=1, source_target_pairs={{0,1},{1,0},{2,3},{3,2},{4,5},{5,4},{6,7},{7,6},{8,9},{9,8},{10,11... | collective-permute-start | bytes 2949128 | tf_op jit(solution)/shard_map/ppermute | solution.py:175
  124.0 24.7 %collective-permute-start.24 = (bf16[2,2,384,128]{3,2,1,0:T(8,128)(2,1)S(1)}, bf16[2,2,384,128]{3,2,1,0:T(8,128)(2,1)S(1)}, u32[]{:S(2)}, u32[]{:S(2)}) collective-permute-start(bf16[2,2,384,128]{3,2,1,0:T(8,128)(2,1)S(1)} %broadcast_select_fusion.6), channel_id=1, source_target_pairs={{0,2},{1,3},{2,0},{3,1},{4,6},{5,7},{6,4},{7,5},{8,10},{9,11},{10,... | collective-permute-start | bytes 1179656 | tf_op jit(solution)/shard_map/ppermute | solution.py:175
  124.4 18.7 %collective-permute-start.22 = (bf16[2,2,384,128]{3,2,1,0:T(8,128)(2,1)S(1)}, bf16[2,2,384,128]{3,2,1,0:T(8,128)(2,1)S(1)}, u32[]{:S(2)}, u32[]{:S(2)}) collective-permute-start(bf16[2,2,384,128]{3,2,1,0:T(8,128)(2,1)S(1)} %broadcast_select_fusion.7), channel_id=1, source_target_pairs={{0,2},{1,3},{2,0},{3,1},{4,6},{5,7},{6,4},{7,5},{8,10},{9,11},{10,... | collective-permute-start | bytes 1179656 | tf_op jit(solution)/shard_map/ppermute | solution.py:175
  130.3 5.4 %collective-permute-start.26 = (bf16[2,2,192,128]{3,2,1,0:T(8,128)(2,1)S(1)}, bf16[2,2,192,128]{3,2,1,0:T(8,128)(2,1)S(1)}, u32[]{:S(2)}, u32[]{:S(2)}) collective-permute-start(bf16[2,2,192,128]{3,2,1,0:T(8,128)(2,1)S(1)} %get-tuple-element.100), channel_id=1, source_target_pairs={{0,1},{1,0},{2,3},{3,2},{4,5},{5,4},{6,7},{7,6},{8,9},{9,8},{10,11... | collective-permute-start | bytes 589832 | tf_op jit(solution)/shard_map/ppermute | solution.py:175
  135.7 17.7 %collective-permute-start.27 = (bf16[2,2,192,128]{3,2,1,0:T(8,128)(2,1)S(1)}, bf16[2,2,192,128]{3,2,1,0:T(8,128)(2,1)S(1)}, u32[]{:S(2)}, u32[]{:S(2)}) collective-permute-start(bf16[2,2,192,128]{3,2,1,0:T(8,128)(2,1)S(1)} %get-tuple-element.98), channel_id=1, source_target_pairs={{0,1},{1,0},{2,3},{3,2},{4,5},{5,4},{6,7},{7,6},{8,9},{9,8},{10,11... | collective-permute-start | bytes 589832 | tf_op jit(solution)/shard_map/ppermute | solution.py:175
  147.7 5.8 %collective-permute-start.28 = (bf16[2,2,192,128]{3,2,1,0:T(8,128)(2,1)S(1)}, bf16[2,2,192,128]{3,2,1,0:T(8,128)(2,1)S(1)}, u32[]{:S(2)}, u32[]{:S(2)}) collective-permute-start(bf16[2,2,192,128]{3,2,1,0:T(8,128)(2,1)S(1)} %get-tuple-element.96), channel_id=1, source_target_pairs={{0,1},{1,0},{2,3},{3,2},{4,5},{5,4},{6,7},{7,6},{8,9},{9,8},{10,11... | collective-permute-start | bytes 589832 | tf_op jit(solution)/shard_map/ppermute | solution.py:175
  153.3 1.5 collective-permute-start.29
  (2 other events, 3.5 us)
where the time goes:
time: 159 us; the launch traced here: 158 us
  starting transfers between devices  64.2 us (40%)
  Pallas kernels  44.4 us (28%)
  waiting for transfers between devices  35.1 us (22%)
  other arithmetic  10.2 us (6%)
  local copies, waits for them, and re-layouts  2.87 us (2%)
    ppermute x19, starting transfers between devices, swapped(): return lax.ppermute(x, AXES, [(i, i ^ bit) for i in range(count)])  32.1 us
    ppermute x11, starting transfers between devices, shifted(): lax.ppermute(x, AXES, [(i, i + by) for i in range(count) if 0 <= i + by <...  32.1 us
    pallas_call x5, Pallas kernels, attend_backward(): pl.pallas_call(functools.partial(backward_kernel, scale=scale), grid=(hea...  22.4 us
    pallas_call x5, Pallas kernels, attend_forward(): pl.pallas_call(functools.partial(forward_kernel, scale=scale), grid=(head...  22 us
    ppermute x11, waiting for transfers between devices, shifted(): lax.ppermute(x, AXES, [(i, i + by) for i in range(count) if 0 <= i + by <...  20.2 us
    ppermute x19, waiting for transfers between devices, swapped(): return lax.ppermute(x, AXES, [(i, i ^ bit) for i in range(count)])  14.9 us
  transfers between devices with their start and end apart: 30, of which 8 were waited for; matrix products, arithmetic and copies ran while one was open for 5% of the time, Pallas kernels for 28%

commit v1 on v0

v1 whole, which is shorter than its diff:
```python
import functools
import math

import jax
import jax.numpy as jnp
from jax import lax
from jax.experimental import pallas as pl
from jax.experimental.pallas import tpu as pltpu
from jax.sharding import PartitionSpec as P

FRAME = 64
AXES = ("ctx", "head")
GROUP = 4
MASKED = -1e30
KEY_CHUNKS = (3, 4, 3)
QUERY_CHUNKS = (4, 3, 2, 1)
FAR_IN_FLIGHT = 2
NEAR_IN_FLIGHT = 2
FORWARD_LEAD = 3
BACKWARD_LEAD = 3
OUTPUT_LEAD = 2
QUERY_TIE = 3
KERNEL_LAG = 0
COST = 1.0
VMEM = 16 * 2**20
SMALL = 8 * 2**20
NT = ((1,), (1,))
NN = ((1,), (0,))


def dot(a, b, dims):
    return lax.dot_general(a, b, (dims, ((), ())), preferred_element_type=jnp.float32)


def starts(sizes):
    return [sum(sizes[:i]) for i in range(len(sizes))]


def by_core(scratch, keep_ref, send_ref, core):
    rows = keep_ref.shape[2]
    mine = pl.multiple_of(core * rows, rows)
    other = pl.multiple_of((1 - core) * rows, rows)
    keep_ref[:, 0] = scratch[:, pl.ds(mine, rows), :]
    send_ref[:, 0] = scratch[:, pl.ds(other, rows), :]


def forward_kernel(
    where_ref, q_ref, kv0_ref, kv1_ref, kv2_ref, near_ref, docs_ref, keep_ref, send_ref, stat_ref, done, *, scale
):
    span = q_ref.shape[2]
    factor = scale * math.log2(math.e)
    core = where_ref[1]
    query, grad = q_ref[0, 0], q_ref[1, 0]
    doc_col, limit_col = near_ref[:, 0:1], near_ref[:, 1:2]
    segments = ((kv2_ref[0, 0], kv2_ref[1, 0]), (kv1_ref[0, 0], kv1_ref[1, 0]), (kv0_ref[0, 0], kv0_ref[1, 0]))
    scores = []
    for i, (key, _) in enumerate(segments):
        raw = dot(query, key, NT) * factor
        allowed = docs_ref[:, i * span : (i + 1) * span] == doc_col
        if i == 2:
            place = lax.broadcasted_iota(jnp.int32, raw.shape, 1)
            allowed = allowed & (place <= limit_col)
        scores.append(jnp.where(allowed, raw, MASKED))
    top = functools.reduce(jnp.maximum, [jnp.max(s, axis=1, keepdims=True) for s in scores])
    raised = [jnp.exp2(s - top) for s in scores]
    total = functools.reduce(jnp.add, [jnp.sum(r, axis=1, keepdims=True) for r in raised])
    inverse = 1.0 / total
    probs = [r * inverse for r in raised]
    mixed = functools.reduce(
        jnp.add, [dot(p.astype(jnp.bfloat16), value, NN) for (_, value), p in zip(segments, probs)]
    )
    output = mixed.astype(jnp.bfloat16)
    delta = jnp.sum(grad.astype(jnp.float32) * output.astype(jnp.float32), axis=1, keepdims=True)
    grad_query = jnp.zeros_like(mixed)
    for (key, value), p in zip(segments, probs):
        grad_score = (p * (dot(grad, value, NT) - delta)).astype(jnp.bfloat16)
        grad_query += dot(grad_score, key, NN)
    done[0] = output
    done[1] = (grad_query * scale).astype(jnp.bfloat16)
    for i, column in enumerate((top + jnp.log2(total), delta)):
        stat_ref[0, i : i + 1, :] = jnp.broadcast_to(column, (span, 128)).T[0:1]
    by_core(done, keep_ref, send_ref, core)


def backward_kernel(
    where_ref, kv_ref, q0_ref, q1_ref, q2_ref, st0_ref, st1_ref, st2_ref, rows_ref, near_ref, keep_ref, send_ref, done, *, scale
):
    span = kv_ref.shape[2]
    factor = scale * math.log2(math.e)
    core = where_ref[1]
    key, value = kv_ref[0, 0], kv_ref[1, 0]
    key_doc = near_ref[:, 0:1]
    grad_key = jnp.zeros(key.shape, jnp.float32)
    grad_value = jnp.zeros(key.shape, jnp.float32)
    segments = (
        (q0_ref[0, 0], q0_ref[1, 0], st0_ref),
        (q1_ref[0, 0], q1_ref[1, 0], st1_ref),
        (q2_ref[0, 0], q2_ref[1, 0], st2_ref),
    )
    for i, (query, grad, stats) in enumerate(segments):
        raw = dot(key, query, NT) * factor
        allowed = key_doc == rows_ref[0:1, i * span : (i + 1) * span]
        if i == 0:
            place = lax.broadcasted_iota(jnp.int32, raw.shape, 0)
            allowed = allowed & (place <= rows_ref[1:2, :span])
        probs = jnp.exp2(jnp.where(allowed, raw - stats[0, 0:1], MASKED))
        grad_value += dot(probs.astype(jnp.bfloat16), grad, NN)
        grad_prob = dot(value, grad, NT)
        grad_score = (probs * (grad_prob - stats[0, 1:2])).astype(jnp.bfloat16)
        grad_key += dot(grad_score, query, NN)
    done[0] = (grad_key * scale).astype(jnp.bfloat16)
    done[1] = grad_value.astype(jnp.bfloat16)
    by_core(done, keep_ref, send_ref, core)


def per_head(shape, start=0):
    return pl.BlockSpec((shape[0], 1) + shape[2:], lambda h: (0, h + start, 0, 0))


def per_head_stats(shape, start=0):
    return pl.BlockSpec((1,) + shape[1:], lambda h: (h + start, 0, 0))


def whole(shape):
    return pl.BlockSpec(shape, lambda h: (0,) * len(shape))


def cost(heads, span, dim):
    pairs = heads * span * span * 3
    return pl.CostEstimate(
        flops=int(COST * 2 * pairs * dim * 4), bytes_accessed=int(COST * heads * span * dim * 2 * 10), transcendentals=int(COST * pairs)
    )


def attend(kernel, heads, here, arrays, stats, tables, scale, gives_stats):
    _, _, span, dim = arrays[0][0].shape
    shape = (2, heads, span // 2, dim)
    out_specs = [per_head(shape), per_head(shape)]
    out_shape = [jax.ShapeDtypeStruct(shape, jnp.bfloat16)] * 2
    if gives_stats:
        out_specs.append(per_head_stats((heads, 2, span)))
        out_shape.append(jax.ShapeDtypeStruct((heads, 2, span), jnp.float32))
    return pl.pallas_call(
        functools.partial(kernel, scale=scale),
        grid=(heads,),
        in_specs=[pl.BlockSpec(memory_space=pltpu.SMEM)]
        + [per_head(x.shape, first) for x, first in arrays]
        + [per_head_stats(x.shape, first) for x, first in stats]
        + [whole(x.shape) for x in tables],
        out_specs=out_specs,
        out_shape=out_shape,
        scratch_shapes=[pltpu.VMEM((2, span, dim), jnp.bfloat16)],
        compiler_params=pltpu.CompilerParams(vmem_limit_bytes=VMEM),
        cost_estimate=cost(heads, span, dim),
    )(here, *[x for x, _ in arrays], *[x for x, _ in stats], *tables)


def finish(copies, sems):
    running = [pltpu.make_async_copy(a, b, sems.at[i]) for i, (a, b) in enumerate(copies)]
    for c in running:
        c.start()
    for c in running:
        c.wait()


def laid_out(where_ref, x_ref, y_ref, came_ref, *rest, cuts):
    parts, staged, sems = rest[:-2], rest[-2], rest[-1]
    core = where_ref[1]
    half, rows = came_ref.shape[1], came_ref.shape[2]
    mine = pl.multiple_of(core * rows, rows)
    other = pl.multiple_of((1 - core) * rows, rows)
    own = pl.ds(core * half, half)
    finish(
        [
            (x_ref.at[own], staged.at[0, :, pl.ds(mine, rows)]),
            (y_ref.at[own], staged.at[1, :, pl.ds(mine, rows)]),
            (came_ref, staged.at[:, :, pl.ds(other, rows)]),
        ],
        sems,
    )
    finish([(staged.at[:, pl.ds(at, size)], part) for part, (at, size) in zip(parts, cuts)], sems)


def lay_out(here, x, y, came, cuts):
    half, rows, dim = came.shape[1:]
    return pl.pallas_call(
        functools.partial(laid_out, cuts=cuts),
        in_specs=[pl.BlockSpec(memory_space=pltpu.SMEM)]
        + [pl.BlockSpec(memory_space=pltpu.HBM)] * 2
        + [pl.BlockSpec(memory_space=pl.ANY)],
        out_specs=[pl.BlockSpec(memory_space=pl.ANY)] * len(cuts),
        out_shape=[jax.ShapeDtypeStruct((2, n, 2 * rows, dim), x.dtype) for _, n in cuts],
        scratch_shapes=[pltpu.VMEM((2, half, 2 * rows, dim), x.dtype), pltpu.SemaphoreType.DMA((3 + len(cuts),))],
        compiler_params=pltpu.CompilerParams(vmem_limit_bytes=SMALL),
        cost_estimate=pl.CostEstimate(flops=0, bytes_accessed=8 * half * rows * dim * 2, transcendentals=0),
    )(here, x, y, came)


def gathered(where_ref, *refs, sizes):
    n = len(sizes)
    kept, came, results, sems = refs[:n], refs[n : 2 * n], refs[2 * n : 2 * n + 2], refs[-1]
    core = where_ref[1]
    half = sum(sizes)
    copies = []
    for j, (begin, size) in enumerate(zip(starts(sizes), sizes)):
        for i, to in enumerate(results):
            copies.append((kept[j].at[i], to.at[pl.ds(core * half + begin, size)]))
            copies.append((came[j].at[i], to.at[pl.ds((1 - core) * half + begin, size)]))
    finish(copies, sems)


def gather(here, kept, came):
    sizes = tuple(k.shape[1] for k in kept)
    _, _, rows, dim = kept[0].shape
    shape = (2 * sum(sizes), rows, dim)
    return pl.pallas_call(
        functools.partial(gathered, sizes=sizes),
        in_specs=[pl.BlockSpec(memory_space=pltpu.SMEM)] + [pl.BlockSpec(memory_space=pltpu.VMEM)] * (2 * len(sizes)),
        out_specs=[pl.BlockSpec(memory_space=pltpu.HBM)] * 2,
        out_shape=[jax.ShapeDtypeStruct(shape, kept[0].dtype)] * 2,
        scratch_shapes=[pltpu.SemaphoreType.DMA((4 * len(sizes),))],
        compiler_params=pltpu.CompilerParams(vmem_limit_bytes=SMALL),
        cost_estimate=pl.CostEstimate(flops=0, bytes_accessed=8 * sum(sizes) * rows * dim * 2, transcendentals=0),
    )(here, *kept, *came)


def tied(x, *after):
    return lax.optimization_barrier((x,) + after)[0] if after else x


def local(query_in, key_in, value_in, grad_out, doc_ids, frame_kind):
    rows_own, heads, dim = query_in.shape
    half = heads // 2
    span = 2 * rows_own
    count = lax.axis_size("ctx") * lax.axis_size("head")
    at = lax.axis_index("ctx") * lax.axis_size("head") + lax.axis_index("head")
    core = at % 2
    side = (at // 2) % 2
    base = (at - core) * rows_own
    scale = dim**-0.5
    here = jnp.stack([side, core]).astype(jnp.int32)

    def sent(x, pairs, name):
        with jax.named_scope(name):
            return lax.ppermute(x, AXES, [(i, j) for i, j in pairs if 0 <= j < count])

    ahead = [(i, i + GROUP) for i in range(count)]
    behind = [(i, i - GROUP) for i in range(count)]
    across = [(i, i ^ 1) for i in range(count)]
    beside = [(i, i ^ 2) for i in range(count)]
    before = [(i, i - 2) for i in range(count)]

    by_head = [x.transpose(1, 0, 2) for x in (key_in, value_in, query_in, grad_out)]

    def theirs(x, y):
        return jnp.stack([lax.dynamic_slice_in_dim(a, (1 - core) * half, half, 0) for a in (x, y)])

    key_cuts = tuple(zip(starts(KEY_CHUNKS), KEY_CHUNKS))
    query_cuts = tuple(zip(starts(QUERY_CHUNKS), QUERY_CHUNKS))
    edges = sorted({a for a, _ in key_cuts + query_cuts}) + [half]
    calls = tuple((a, b - a) for a, b in zip(edges[:-1], edges[1:]))
    nk, nq = len(KEY_CHUNKS), len(QUERY_CHUNKS)
    came_kv = sent(theirs(*by_head[:2]), across, "pair_kv")
    kv_parts = lay_out(here, *by_head[:2], came_kv, key_cuts)
    came_q = sent(tied(theirs(*by_head[2:]), came_kv), across, "pair_q")
    q_parts = lay_out(here, *by_head[2:], came_q, query_cuts)

    doc_ids, frame_kind = tied((doc_ids, frame_kind), came_q)
    reach = 2 * span
    docs = jnp.concatenate(
        [jnp.full((reach,), -1, jnp.int32), doc_ids, jnp.full((reach,), -2, jnp.int32)]
    )
    docs = lax.dynamic_slice_in_dim(docs, base, 5 * span)
    kinds = jnp.concatenate([frame_kind, jnp.zeros((reach // FRAME,), jnp.int32)])
    kinds = lax.dynamic_slice_in_dim(kinds, base // FRAME, 3 * span // FRAME)
    place = jnp.arange(3 * span, dtype=jnp.int32)
    limit = jnp.where(jnp.repeat(kinds, FRAME) == 1, (place // FRAME) * FRAME + FRAME - 1, place)
    rows = jnp.stack([docs[reach:], limit])
    near_docs = rows[:, :span].T
    key_docs = docs[None, : 3 * span]

    def part(parts, cuts, start):
        k = max(i for i, (first, _) in enumerate(cuts) if first <= start)
        return parts[k], start - cuts[k][0]

    def ready(cuts, count):
        have = sum(size for _, size in cuts[:count])
        return [i for i, (start, size) in enumerate(calls) if start + size <= have]

    far = []
    for j, piece in enumerate(kv_parts + q_parts):
        after = [far[j - FAR_IN_FLIGHT]] if j >= FAR_IN_FLIGHT else []
        if j == QUERY_TIE and 0 < j < nk:
            after.append(q_parts[0])
        far.append(sent(tied(piece, *after), ahead if j < nk else behind, f"far_{j}"))
    near, forward, backward, results, kept = [], [], [], [], []
    for j, piece in enumerate(kv_parts + q_parts):
        first, second = (piece, far[j]) if j < nk else (far[j], piece)
        after = [near[j - NEAR_IN_FLIGHT]] if j >= NEAR_IN_FLIGHT else []
        if FORWARD_LEAD:
            after += [forward[i][0] for i in ready(key_cuts, max(0, j + 1 - FORWARD_LEAD))]
        if BACKWARD_LEAD:
            after += [backward[i][0] for i in ready(query_cuts, max(0, j + 1 - nk - BACKWARD_LEAD))]
        if OUTPUT_LEAD and j >= nk + nq - OUTPUT_LEAD:
            after += results
        near.append(sent(tied(jnp.where(side == 0, first, second), *after), beside, f"near_{j}"))
        for i in ready(key_cuts, min(j + 1, nk))[len(forward) :]:
            start, size = calls[i]
            arrays = [part(q_parts, query_cuts, start)]
            arrays += [part(x, key_cuts, start) for x in (kv_parts, near, far)]
            if KERNEL_LAG:
                x, at_head = arrays[2]
                arrays[2] = (tied(x, far[min(j + KERNEL_LAG, nk + nq - 1)]), at_head)
            forward.append(attend(forward_kernel, size, here, arrays, [], [near_docs, key_docs], scale, True))
        if len(forward) == len(calls) and not kept:
            st0 = jnp.concatenate([f[2] for f in forward], axis=0)
            kept = [st0, sent(st0, before, "next_stats"), sent(st0, behind, "far_stats")]
            results = gather(here, [p[0] for p in forward], [sent(p[1], across, "pair_out") for p in forward])
        if j >= nk:
            for i in ready(query_cuts, j + 1 - nk)[len(backward) :]:
                start, size = calls[i]
                arrays = [part(kv_parts, key_cuts, start)]
                arrays += [part(x, query_cuts, start) for x in (q_parts, near[nk:], far[nk:])]
                if KERNEL_LAG:
                    x, at_head = arrays[2]
                    arrays[2] = (tied(x, far[min(j + KERNEL_LAG, nk + nq - 1)]), at_head)
                stats = [(x, start) for x in kept]
                backward.append(attend(backward_kernel, size, here, arrays, stats, [rows, near_docs], scale, False))

    results = list(results) + list(
        gather(here, [p[0] for p in backward], [sent(p[1], across, "pair_out") for p in backward])
    )
    return tuple(x.transpose(1, 0, 2) for x in results)


def solution(mesh):
    placed = P(AXES, None, None)
    return jax.shard_map(
        local,
        mesh=mesh,
        in_specs=(placed,) * 4 + (P(), P()),
        out_specs=(placed,) * 4,
        check_vma=False,
    )
```

time: 159 us -> 151 us (0.950)
  starting transfers between devices: 64.2 us -> 53.1 us
  Pallas kernels: 44.4 us -> 49.9 us
  other arithmetic: 10.2 us -> 5.53 us
  local copies, waits for them, and re-layouts: 2.87 us -> 5.15 us
    ppermute x30 -> x28, starting transfers between devices: 64.2 us -> 53.1 us  [sent(): return lax.ppermute(x, AXES, [(i, j) for i, j in pairs if 0 <= j < count])]
    pallas_call x10 -> x14, Pallas kernels: 44.4 us -> 49.9 us  [the longest x10 40.9 us: attend(): pl.pallas_call(functools.partial(kernel, scale=scale), grid=(heads,), in_...]
    unnamed x20 -> x28, local copies, waits for them, and re-layouts: 0.46 us -> 3.5 us
    transpose x2 -> x0, other arithmetic: 2.89 us -> none  [returned(): return (both[0].transpose(1, 0, 2), both[1].transpose(1, 0, 2))]
    select_n x23 -> x7, other arithmetic: 4.75 us -> 3.19 us  [local(): jnp.where(side == 0, first, second)]
    ppermute x30 -> x28, waiting for transfers between devices: 35.1 us -> 34.6 us  [sent(): return lax.ppermute(x, AXES, [(i, j) for i, j in pairs if 0 <= j < count])]
  transfers between devices with their start and end apart: 30 -> 28, of which waited for: 8 -> 7; matrix products, arithmetic and copies ran while one was open for 5% -> 3% of each run, Pallas kernels for 28% -> 30%
where the time goes in v1:
time: 151 us; the launch traced here: 150 us
  starting transfers between devices  53.1 us (35%)
  Pallas kernels  49.9 us (33%)
  waiting for transfers between devices  34.6 us (23%)
  other arithmetic  5.53 us (4%)
  local copies, waits for them, and re-layouts  5.15 us (3%)
    ppermute x28, starting transfers between devices, sent(): return lax.ppermute(x, AXES, [(i, j) for i, j in pairs if 0 <= j < count])  53.1 us
    pallas_call x10, Pallas kernels, attend(): pl.pallas_call(functools.partial(kernel, scale=scale), grid=(heads,), in_...  40.9 us
    ppermute x28, waiting for transfers between devices, sent(): return lax.ppermute(x, AXES, [(i, j) for i, j in pairs if 0 <= j < count])  34.6 us
    pallas_call x2, Pallas kernels, lay_out(): pl.pallas_call(functools.partial(laid_out, cuts=cuts), in_specs=[pl.Block...  5 us
    pallas_call x2, Pallas kernels, gather(): pl.pallas_call(functools.partial(gathered, sizes=sizes), in_specs=[pl.Blo...  3.94 us
    unnamed x28, local copies, waits for them, and re-layouts  3.5 us
    select_n x7, other arithmetic, local(): jnp.where(side == 0, first, second)  3.19 us
  transfers between devices with their start and end apart: 28, of which 7 were waited for; matrix products, arithmetic and copies ran while one was open for 3% of the time, Pallas kernels for 30%

profile of v1, /device:TPU:27, one launch (start us, length us, event | category | flops | bytes accessed | tf_op | source)
XLA Modules:
  0.0 149.6 jit_solution(16370569404452184124)
XLA Ops:
  0.7 1.2 dynamic-slice_bitcast_fusion
  3.7 2.5 %collective-permute-done.came_ref = bf16[2,10,192,128]{3,2,1,0:T(8,128)(2,1)} collective-permute-done((bf16[2,10,192,128]{3,2,1,0:T(8,128)(2,1)}, bf16[2,10,192,128]{3,2,1,0:T(8,128)(2,1)}, u32[]{:S(2)}, u32[]{:S(2)}) %collective-permute-start) | collective-permute-done | bytes 983072 | tf_op jit(solution)/shard_map/pair_kv/ppermute | solution.py:245
  6.2 2.7 %shard_map.94 = (bf16[2,3,384,128]{3,2,1,0:T(8,128)(2,1)}, bf16[2,4,384,128]{3,2,1,0:T(8,128)(2,1)S(1)}, bf16[2,3,384,128]{3,2,1,0:T(8,128)(2,1)S(1)}) custom-call(s32[2]{0:T(128)S(1)} %pad_add_fusion.1.where_ref, bf16[20,192,128]{2,1,0:T(8,128)(2,1)S(1)} %bitcast.37, bf16[20,192,128]{2,1,0:T(8,128)(2,1)S(1)} %bitcast.38, ...), custom_call_target="tpu_custom_call" | custom-call | bytes 3932160 | tf_op jit(solution)/shard_map/pallas_call | solution.py:186
  8.9 1.3 collective-permute-start.2
  10.3 1.3 collective-permute-start.4
  13.0 12.5 %collective-permute-done.2.kv2_ref = bf16[2,3,384,128]{3,2,1,0:T(8,128)(2,1)S(1)} collective-permute-done((bf16[2,3,384,128]{3,2,1,0:T(8,128)(2,1)}, bf16[2,3,384,128]{3,2,1,0:T(8,128)(2,1)S(1)}, u32[]{:S(2)}, u32[]{:S(2)}) %collective-permute-start.2) | collective-permute-done | bytes 589856 | tf_op jit(solution)/shard_map/far_0/ppermute | solution.py:245
  25.6 1.9 %broadcast_select_fusion.4 = bf16[2,3,384,128]{3,2,1,0:T(8,128)(2,1)} fusion(bf16[2,3,384,128]{3,2,1,0:T(8,128)(2,1)} %get-tuple-element.55.kv0_ref.kv_ref, bf16[2,3,384,128]{3,2,1,0:T(8,128)(2,1)S(1)} %collective-permute-done.2.kv2_ref, pred[]{:T(512)S(6)} %eq.26), kind=kLoop, calls=%fused_computation.6 | loop fusion | flops 294912 | bytes 1769473 | tf_op jit(solution)/shard_map/jit(_where)/select_n | solution.py:306
  27.7 1.3 collective-permute-start.6
  29.0 13.5 %collective-permute-done.4.kv2_ref = bf16[2,4,384,128]{3,2,1,0:T(8,128)(2,1)S(1)} collective-permute-done((bf16[2,4,384,128]{3,2,1,0:T(8,128)(2,1)S(1)}, bf16[2,4,384,128]{3,2,1,0:T(8,128)(2,1)S(1)}, u32[]{:S(2)}, u32[]{:S(2)}) %collective-permute-start.4) | collective-permute-done | bytes 786464 | tf_op jit(solution)/shard_map/far_1/ppermute | solution.py:245
  48.6 2.3 %shard_map.93 = (bf16[2,4,384,128]{3,2,1,0:T(8,128)(2,1)S(1)}, bf16[2,3,384,128]{3,2,1,0:T(8,128)(2,1)S(1)}, bf16[2,2,384,128]{3,2,1,0:T(8,128)(2,1)S(1)}, bf16[2,1,384,128]{3,2,1,0:T(8,128)(2,1)S(1)}) custom-call(s32[2]{0:T(128)S(1)} %pad_add_fusion.1.where_ref, bf16[20,192,128]{2,1,0:T(8,128)(2,1)S(1)} %bitcast.39, bf16[20,192,128]{2,1,0:T(8,128)(2,1)S(1)} %bitcast.40, ...), custom_call_target="tpu_custom_call" | custom-call | bytes 3932160 | tf_op jit(solution)/shard_map/pallas_call | solution.py:186
  50.9 3.1 %collective-permute-start.13 = (bf16[2,4,384,128]{3,2,1,0:T(8,128)(2,1)S(1)}, bf16[2,4,384,128]{3,2,1,0:T(8,128)(2,1)S(1)}, u32[]{:S(2)}, u32[]{:S(2)}) collective-permute-start(bf16[2,4,384,128]{3,2,1,0:T(8,128)(2,1)S(1)} %get-tuple-element.77.q_ref.q0_ref), channel_id=1, source_target_pairs={{4,0},{5,1},{6,2},{7,3},{8,4},{9,5},{10,6},{11,7},{12,8},{13,9},{1... | collective-permute-start | bytes 2359304 | tf_op jit(solution)/shard_map/far_3/ppermute | solution.py:245
  54.1 6.7 %shard_map.95 = (bf16[2,3,192,128]{3,2,1,0:T(8,128)(2,1)S(1)}, bf16[2,3,192,128]{3,2,1,0:T(8,128)(2,1)S(1)}, f32[3,2,384]{2,1,0:T(2,128)S(1)}) custom-call(s32[2]{0:T(128)S(1)} %pad_add_fusion.1.where_ref, bf16[2,4,384,128]{3,2,1,0:T(8,128)(2,1)S(1)} %get-tuple-element.77.q_ref.q0_ref, bf16[2,3,384,128]{3,2,1,0:T(8,128)(2,1)} %get-tuple-element.55.kv0_ref.kv_ref, ...), custom_call_target="tpu_custom_call" | custom-call | flops 1358954496 | bytes 2949120 | tf_op jit(solution)/shard_map/pallas_call | solution.py:143
  60.8 2.6 %collective-permute-start.8 = (bf16[2,3,192,128]{3,2,1,0:T(8,128)(2,1)S(1)}, bf16[2,3,192,128]{3,2,1,0:T(8,128)(2,1)S(1)}, u32[]{:S(2)}, u32[]{:S(2)}) collective-permute-start(bf16[2,3,192,128]{3,2,1,0:T(8,128)(2,1)S(1)} %get-tuple-element.70), channel_id=1, source_target_pairs={{0,1},{1,0},{2,3},{3,2},{4,5},{5,4},{6,7},{7,6},{8,9},{9,8},{10,11... | collective-permute-start | bytes 884744 | tf_op jit(solution)/shard_map/pair_out/ppermute | solution.py:245
  63.8 2.1 %collective-permute-start.17 = (bf16[2,3,384,128]{3,2,1,0:T(8,128)(2,1)S(1)}, bf16[2,3,384,128]{3,2,1,0:T(8,128)(2,1)S(1)}, u32[]{:S(2)}, u32[]{:S(2)}) collective-permute-start(bf16[2,3,384,128]{3,2,1,0:T(8,128)(2,1)S(1)} %get-tuple-element.86.q_ref.q0_ref), channel_id=1, source_target_pairs={{4,0},{5,1},{6,2},{7,3},{8,4},{9,5},{10,6},{11,7},{12,8},{13,9},{1... | collective-permute-start | bytes 1769480 | tf_op jit(solution)/shard_map/far_4/ppermute | solution.py:245
  65.9 2.8 %shard_map.96 = (bf16[2,1,192,128]{3,2,1,0:T(8,128)(2,1)S(1)}, bf16[2,1,192,128]{3,2,1,0:T(8,128)(2,1)S(1)}, f32[1,2,384]{2,1,0:T(2,128)S(1)}) custom-call(s32[2]{0:T(128)S(1)} %pad_add_fusion.1.where_ref, bf16[2,4,384,128]{3,2,1,0:T(8,128)(2,1)S(1)} %get-tuple-element.77.q_ref.q0_ref, bf16[2,4,384,128]{3,2,1,0:T(8,128)(2,1)S(1)} %get-tuple-element.59.kv0_ref.kv_ref, ...), custom_call_target="tpu_custom_call" | custom-call | flops 452984832 | bytes 983040 | tf_op jit(solution)/shard_map/pallas_call | solution.py:143
  69.4 6.6 %shard_map.97 = (bf16[2,3,192,128]{3,2,1,0:T(8,128)(2,1)S(1)}, bf16[2,3,192,128]{3,2,1,0:T(8,128)(2,1)S(1)}, f32[3,2,384]{2,1,0:T(2,128)S(1)}) custom-call(s32[2]{0:T(128)S(1)} %pad_add_fusion.1.where_ref, bf16[2,3,384,128]{3,2,1,0:T(8,128)(2,1)S(1)} %get-tuple-element.86.q_ref.q0_ref, bf16[2,4,384,128]{3,2,1,0:T(8,128)(2,1)S(1)} %get-tuple-element.59.kv0_ref.kv_ref, ...), custom_call_target="tpu_custom_call" | custom-call | flops 1358954496 | bytes 2949120 | tf_op jit(solution)/shard_map/pallas_call | solution.py:143
  76.0 20.3 %collective-permute-start.19 = (bf16[2,2,384,128]{3,2,1,0:T(8,128)(2,1)S(1)}, bf16[2,2,384,128]{3,2,1,0:T(8,128)(2,1)S(1)}, u32[]{:S(2)}, u32[]{:S(2)}) collective-permute-start(bf16[2,2,384,128]{3,2,1,0:T(8,128)(2,1)S(1)} %get-tuple-element.89.q_ref.q0_ref), channel_id=1, source_target_pairs={{4,0},{5,1},{6,2},{7,3},{8,4},{9,5},{10,6},{11,7},{12,8},{13,9},{1... | collective-permute-start | bytes 1179656 | tf_op jit(solution)/shard_map/far_5/ppermute | solution.py:245
  97.0 2.4 %shard_map.99 = (bf16[2,1,192,128]{3,2,1,0:T(8,128)(2,1)S(1)}, bf16[2,1,192,128]{3,2,1,0:T(8,128)(2,1)S(1)}, f32[1,2,384]{2,1,0:T(2,128)S(1)}) custom-call(s32[2]{0:T(128)S(1)} %pad_add_fusion.1.where_ref, bf16[2,1,384,128]{3,2,1,0:T(8,128)(2,1)S(1)} %get-tuple-element.92.q_ref.q0_ref, bf16[2,3,384,128]{3,2,1,0:T(8,128)(2,1)S(1)} %get-tuple-element.65.kv0_ref.kv_ref, ...), custom_call_target="tpu_custom_call" | custom-call | flops 452984832 | bytes 983040 | tf_op jit(solution)/shard_map/pallas_call | solution.py:143
  99.3 4.3 %shard_map.98 = (bf16[2,2,192,128]{3,2,1,0:T(8,128)(2,1)S(1)}, bf16[2,2,192,128]{3,2,1,0:T(8,128)(2,1)S(1)}, f32[2,2,384]{2,1,0:T(2,128)S(1)}) custom-call(s32[2]{0:T(128)S(1)} %pad_add_fusion.1.where_ref, bf16[2,2,384,128]{3,2,1,0:T(8,128)(2,1)S(1)} %get-tuple-element.89.q_ref.q0_ref, bf16[2,3,384,128]{3,2,1,0:T(8,128)(2,1)S(1)} %get-tuple-element.65.kv0_ref.kv_ref, ...), custom_call_target="tpu_custom_call" | custom-call | flops 905969664 | bytes 1966080 | tf_op jit(solution)/shard_map/pallas_call | solution.py:143
  104.3 1.7 %collective-permute-start.16 = (f32[10,2,384]{2,1,0:T(2,128)S(1)}, f32[10,2,384]{2,1,0:T(2,128)S(1)}, u32[]{:S(2)}, u32[]{:S(2)}) collective-permute-start(f32[10,2,384]{2,1,0:T(2,128)S(1)} %constant_dynamic-update-slice_fusion.st0_ref), channel_id=1, source_target_pairs={{4,0},{5,1},{6,2},{7,3},{8,4},{9,5},{10,6},{11,7},{12,8},{13,9},{1... | collective-permute-start | bytes 92168 | tf_op jit(solution)/shard_map/far_stats/ppermute | solution.py:245
  106.0 4.9 %collective-permute-start.15 = (f32[10,2,384]{2,1,0:T(2,128)S(1)}, f32[10,2,384]{2,1,0:T(2,128)S(1)}, u32[]{:S(2)}, u32[]{:S(2)}) collective-permute-start(f32[10,2,384]{2,1,0:T(2,128)S(1)} %constant_dynamic-update-slice_fusion.st0_ref), channel_id=1, source_target_pairs={{2,0},{3,1},{4,2},{5,3},{6,4},{7,5},{8,6},{9,7},{10,8},{11,9},{12,... | collective-permute-start | bytes 92168 | tf_op jit(solution)/shard_map/next_stats/ppermute | solution.py:245
  110.9 1.9 %collective-permute-start.21 = (bf16[2,1,384,128]{3,2,1,0:T(8,128)(2,1)S(1)}, bf16[2,1,384,128]{3,2,1,0:T(8,128)(2,1)S(1)}, u32[]{:S(2)}, u32[]{:S(2)}) collective-permute-start(bf16[2,1,384,128]{3,2,1,0:T(8,128)(2,1)S(1)} %get-tuple-element.92.q_ref.q0_ref), channel_id=1, source_target_pairs={{4,0},{5,1},{6,2},{7,3},{8,4},{9,5},{10,6},{11,7},{12,8},{13,9},{1... | collective-permute-start | bytes 589832 | tf_op jit(solution)/shard_map/far_6/ppermute | solution.py:245
  112.8 2.0 %shard_map.100 = (bf16[20,192,128]{2,1,0:T(8,128)(2,1)}, bf16[20,192,128]{2,1,0:T(8,128)(2,1)}) custom-call(s32[2]{0:T(128)S(1)} %pad_add_fusion.1.where_ref, bf16[2,3,192,128]{3,2,1,0:T(8,128)(2,1)S(1)} %get-tuple-element.58.refs_0_, bf16[2,1,192,128]{3,2,1,0:T(8,128)(2,1)S(1)} %get-tuple-element.60.refs_1_, ...), custom_call_target="tpu_custom_call" | custom-call | bytes 3932160 | tf_op jit(solution)/shard_map/pallas_call | solution.py:216
  116.6 2.0 %shard_map.102 = (bf16[2,1,192,128]{3,2,1,0:T(8,128)(2,1)S(1)}, bf16[2,1,192,128]{3,2,1,0:T(8,128)(2,1)S(1)}) custom-call(s32[2]{0:T(128)S(1)} %pad_add_fusion.1.where_ref, bf16[2,4,384,128]{3,2,1,0:T(8,128)(2,1)S(1)} %get-tuple-element.59.kv0_ref.kv_ref, bf16[2,4,384,128]{3,2,1,0:T(8,128)(2,1)S(1)} %get-tuple-element.77.q_ref.q0_ref, ...), custom_call_target="tpu_custom_call" | custom-call | flops 452984832 | bytes 983040 | tf_op jit(solution)/shard_map/pallas_call | solution.py:143
  118.6 5.5 %shard_map.101 = (bf16[2,3,192,128]{3,2,1,0:T(8,128)(2,1)S(1)}, bf16[2,3,192,128]{3,2,1,0:T(8,128)(2,1)S(1)}) custom-call(s32[2]{0:T(128)S(1)} %pad_add_fusion.1.where_ref, bf16[2,3,384,128]{3,2,1,0:T(8,128)(2,1)} %get-tuple-element.55.kv0_ref.kv_ref, bf16[2,4,384,128]{3,2,1,0:T(8,128)(2,1)S(1)} %get-tuple-element.77.q_ref.q0_ref, ...), custom_call_target="tpu_custom_call" | custom-call | flops 1358954496 | bytes 2949120 | tf_op jit(solution)/shard_map/pallas_call | solution.py:143
  124.1 4.9 %collective-permute-done.18.q1_ref = bf16[2,3,384,128]{3,2,1,0:T(8,128)(2,1)S(1)} collective-permute-done((bf16[2,3,384,128]{3,2,1,0:T(8,128)(2,1)S(1)}, bf16[2,3,384,128]{3,2,1,0:T(8,128)(2,1)S(1)}, u32[]{:S(2)}, u32[]{:S(2)}) %collective-permute-start.18) | collective-permute-done | bytes 589856 | tf_op jit(solution)/shard_map/near_4/ppermute | solution.py:245
  129.3 5.1 %shard_map.103 = (bf16[2,3,192,128]{3,2,1,0:T(8,128)(2,1)S(1)}, bf16[2,3,192,128]{3,2,1,0:T(8,128)(2,1)S(1)}) custom-call(s32[2]{0:T(128)S(1)} %pad_add_fusion.1.where_ref, bf16[2,4,384,128]{3,2,1,0:T(8,128)(2,1)S(1)} %get-tuple-element.59.kv0_ref.kv_ref, bf16[2,3,384,128]{3,2,1,0:T(8,128)(2,1)S(1)} %get-tuple-element.86.q_ref.q0_ref, ...), custom_call_target="tpu_custom_call" | custom-call | flops 1358954496 | bytes 2949120 | tf_op jit(solution)/shard_map/pallas_call | solution.py:143
  134.4 3.2 %collective-permute-start.25 = (bf16[2,3,192,128]{3,2,1,0:T(8,128)(2,1)S(1)}, bf16[2,3,192,128]{3,2,1,0:T(8,128)(2,1)S(1)}, u32[]{:S(2)}, u32[]{:S(2)}) collective-permute-start(bf16[2,3,192,128]{3,2,1,0:T(8,128)(2,1)S(1)} %get-tuple-element.97), channel_id=1, source_target_pairs={{0,1},{1,0},{2,3},{3,2},{4,5},{5,4},{6,7},{7,6},{8,9},{9,8},{10,11... | collective-permute-start | bytes 884744 | tf_op jit(solution)/shard_map/pair_out/ppermute | solution.py:245
  137.7 3.6 %shard_map.104 = (bf16[2,2,192,128]{3,2,1,0:T(8,128)(2,1)S(1)}, bf16[2,2,192,128]{3,2,1,0:T(8,128)(2,1)S(1)}) custom-call(s32[2]{0:T(128)S(1)} %pad_add_fusion.1.where_ref, bf16[2,3,384,128]{3,2,1,0:T(8,128)(2,1)S(1)} %get-tuple-element.65.kv0_ref.kv_ref, bf16[2,2,384,128]{3,2,1,0:T(8,128)(2,1)S(1)} %get-tuple-element.89.q_ref.q0_ref, ...), custom_call_target="tpu_custom_call" | custom-call | flops 905969664 | bytes 1966080 | tf_op jit(solution)/shard_map/pallas_call | solution.py:143
  141.3 2.7 %collective-permute-start.26 = (bf16[2,2,192,128]{3,2,1,0:T(8,128)(2,1)S(1)}, bf16[2,2,192,128]{3,2,1,0:T(8,128)(2,1)S(1)}, u32[]{:S(2)}, u32[]{:S(2)}) collective-permute-start(bf16[2,2,192,128]{3,2,1,0:T(8,128)(2,1)S(1)} %get-tuple-element.98), channel_id=1, source_target_pairs={{0,1},{1,0},{2,3},{3,2},{4,5},{5,4},{6,7},{7,6},{8,9},{9,8},{10,11... | collective-permute-start | bytes 589832 | tf_op jit(solution)/shard_map/pair_out/ppermute | solution.py:245
  144.0 2.0 %shard_map.105 = (bf16[2,1,192,128]{3,2,1,0:T(8,128)(2,1)S(1)}, bf16[2,1,192,128]{3,2,1,0:T(8,128)(2,1)S(1)}) custom-call(s32[2]{0:T(128)S(1)} %pad_add_fusion.1.where_ref, bf16[2,3,384,128]{3,2,1,0:T(8,128)(2,1)S(1)} %get-tuple-element.65.kv0_ref.kv_ref, bf16[2,1,384,128]{3,2,1,0:T(8,128)(2,1)S(1)} %get-tuple-element.92.q_ref.q0_ref, ...), custom_call_target="tpu_custom_call" | custom-call | flops 452984832 | bytes 983040 | tf_op jit(solution)/shard_map/pallas_call | solution.py:143
  147.4 2.0 %shard_map.106 = (bf16[20,192,128]{2,1,0:T(8,128)(2,1)}, bf16[20,192,128]{2,1,0:T(8,128)(2,1)}) custom-call(s32[2]{0:T(128)S(1)} %pad_add_fusion.1.where_ref, bf16[2,3,192,128]{3,2,1,0:T(8,128)(2,1)S(1)} %get-tuple-element.84.refs_0_, bf16[2,1,192,128]{3,2,1,0:T(8,128)(2,1)S(1)} %get-tuple-element.85.refs_1_, ...), custom_call_target="tpu_custom_call" | custom-call | bytes 3932160 | tf_op jit(solution)/shard_map/pallas_call | solution.py:216
  (92 shorter events, 15.5 us)
Async XLA Ops:
  1.9 4.3 %copy-start = (bf16[192,20,128]{2,0,1:T(8,128)(2,1)S(1)}, bf16[192,20,128]{2,0,1:T(8,128)(2,1)}, u32[]{:S(2)}) copy-start(bf16[192,20,128]{2,0,1:T(8,128)(2,1)} %param.7) | copy-start | bytes 2949124
  3.0 3.2 %collective-permute-start = (bf16[2,10,192,128]{3,2,1,0:T(8,128)(2,1)}, bf16[2,10,192,128]{3,2,1,0:T(8,128)(2,1)}, u32[]{:S(2)}, u32[]{:S(2)}) collective-permute-start(bf16[2,10,192,128]{3,2,1,0:T(8,128)(2,1)} %pad_maximum_fusion.1), channel_id=1, source_target_pairs={{0,1},{1,0},{2,3},{3,2},{4,5},{5,4},{6,7},{7,6},{8,9},{9,8},{10,11... | collective-permute-start | bytes 2949128 | tf_op jit(solution)/shard_map/pair_kv/ppermute | solution.py:245
  8.9 16.6 %collective-permute-start.2 = (bf16[2,3,384,128]{3,2,1,0:T(8,128)(2,1)}, bf16[2,3,384,128]{3,2,1,0:T(8,128)(2,1)S(1)}, u32[]{:S(2)}, u32[]{:S(2)}) collective-permute-start(bf16[2,3,384,128]{3,2,1,0:T(8,128)(2,1)} %get-tuple-element.55.kv0_ref.kv_ref), channel_id=1, source_target_pairs={{0,4},{1,5},{2,6},{3,7},{4,8},{5,9},{6,10},{7,11},{8,12},{9,13},{1... | collective-permute-start | bytes 1769480 | tf_op jit(solution)/shard_map/far_0/ppermute | solution.py:245
  10.3 32.2 %collective-permute-start.4 = (bf16[2,4,384,128]{3,2,1,0:T(8,128)(2,1)S(1)}, bf16[2,4,384,128]{3,2,1,0:T(8,128)(2,1)S(1)}, u32[]{:S(2)}, u32[]{:S(2)}) collective-permute-start(bf16[2,4,384,128]{3,2,1,0:T(8,128)(2,1)S(1)} %get-tuple-element.59.kv0_ref.kv_ref), channel_id=1, source_target_pairs={{0,4},{1,5},{2,6},{3,7},{4,8},{5,9},{6,10},{7,11},{8,12},{9,13},{1... | collective-permute-start | bytes 2359304 | tf_op jit(solution)/shard_map/far_1/ppermute | solution.py:245
  12.7 32.0 %collective-permute-start.1 = (bf16[2,10,192,128]{3,2,1,0:T(8,128)(2,1)}, bf16[2,10,192,128]{3,2,1,0:T(8,128)(2,1)}, u32[]{:S(2)}, u32[]{:S(2)}) collective-permute-start(bf16[2,10,192,128]{3,2,1,0:T(8,128)(2,1)} %pad_maximum_fusion), channel_id=1, source_target_pairs={{0,1},{1,0},{2,3},{3,2},{4,5},{5,4},{6,7},{7,6},{8,9},{9,8},{10,11... | collective-permute-start | bytes 2949128 | tf_op jit(solution)/shard_map/pair_q/ppermute | solution.py:245
  27.5 17.1 %copy-start.11 = (s32[96]{0:T(128)S(1)}, s32[96]{0:T(128)}, u32[]{:S(2)}) copy-start(s32[96]{0:T(128)} %param.11) | copy-start | bytes 1156
  27.5 26.6 %collective-permute-start.3 = (bf16[2,3,384,128]{3,2,1,0:T(8,128)(2,1)}, bf16[2,3,384,128]{3,2,1,0:T(8,128)(2,1)}, u32[]{:S(2)}, u32[]{:S(2)}) collective-permute-start(bf16[2,3,384,128]{3,2,1,0:T(8,128)(2,1)} %broadcast_select_fusion.4), channel_id=1, source_target_pairs={{0,2},{1,3},{2,0},{3,1},{4,6},{5,7},{6,4},{7,5},{8,10},{9,11},{10,... | collective-permute-start | bytes 1769480 | tf_op jit(solution)/shard_map/near_0/ppermute | solution.py:245
  27.7 35.8 %collective-permute-start.6 = (bf16[2,3,384,128]{3,2,1,0:T(8,128)(2,1)S(1)}, bf16[2,3,384,128]{3,2,1,0:T(8,128)(2,1)S(1)}, u32[]{:S(2)}, u32[]{:S(2)}) collective-permute-start(bf16[2,3,384,128]{3,2,1,0:T(8,128)(2,1)S(1)} %get-tuple-element.65.kv0_ref.kv_ref), channel_id=1, source_target_pairs={{0,4},{1,5},{2,6},{3,7},{4,8},{5,9},{6,10},{7,11},{8,12},{9,13},{1... | collective-permute-start | bytes 1769480 | tf_op jit(solution)/shard_map/far_2/ppermute | solution.py:245
  43.5 22.4 %collective-permute-start.5 = (bf16[2,4,384,128]{3,2,1,0:T(8,128)(2,1)}, bf16[2,4,384,128]{3,2,1,0:T(8,128)(2,1)}, u32[]{:S(2)}, u32[]{:S(2)}) collective-permute-start(bf16[2,4,384,128]{3,2,1,0:T(8,128)(2,1)} %broadcast_select_fusion.1), channel_id=1, source_target_pairs={{0,2},{1,3},{2,0},{3,1},{4,6},{5,7},{6,4},{7,5},{8,10},{9,11},{10,... | collective-permute-start | bytes 2359304 | tf_op jit(solution)/shard_map/near_1/ppermute | solution.py:245
  48.6 5.4 %copy-start.7 = (s32[1,1152]{1,0:T(1,128)S(1)}, s32[1,1152]{1,0:T(1,128)}, u32[]{:S(2)}) copy-start(s32[1,1152]{1,0:T(1,128)} %copy-done.6) | copy-start | bytes 13828
  48.6 5.4 %copy-start.9 = (s32[1,1152]{1,0:T(1,128)S(1)}, s32[1,1152]{1,0:T(1,128)}, u32[]{:S(2)}) copy-start(s32[1,1152]{1,0:T(1,128)} %copy-done.8) | copy-start | bytes 13828
  50.9 25.1 %collective-permute-start.13 = (bf16[2,4,384,128]{3,2,1,0:T(8,128)(2,1)S(1)}, bf16[2,4,384,128]{3,2,1,0:T(8,128)(2,1)S(1)}, u32[]{:S(2)}, u32[]{:S(2)}) collective-permute-start(bf16[2,4,384,128]{3,2,1,0:T(8,128)(2,1)S(1)} %get-tuple-element.77.q_ref.q0_ref), channel_id=1, source_target_pairs={{4,0},{5,1},{6,2},{7,3},{8,4},{9,5},{10,6},{11,7},{12,8},{13,9},{1... | collective-permute-start | bytes 2359304 | tf_op jit(solution)/shard_map/far_3/ppermute | solution.py:245
  60.8 42.9 %collective-permute-start.8 = (bf16[2,3,192,128]{3,2,1,0:T(8,128)(2,1)S(1)}, bf16[2,3,192,128]{3,2,1,0:T(8,128)(2,1)S(1)}, u32[]{:S(2)}, u32[]{:S(2)}) collective-permute-start(bf16[2,3,192,128]{3,2,1,0:T(8,128)(2,1)S(1)} %get-tuple-element.70), channel_id=1, source_target_pairs={{0,1},{1,0},{2,3},{3,2},{4,5},{5,4},{6,7},{7,6},{8,9},{9,8},{10,11... | collective-permute-start | bytes 884744 | tf_op jit(solution)/shard_map/pair_out/ppermute | solution.py:245
  63.5 33.0 %collective-permute-start.7 = (bf16[2,3,384,128]{3,2,1,0:T(8,128)(2,1)S(1)}, bf16[2,3,384,128]{3,2,1,0:T(8,128)(2,1)S(1)}, u32[]{:S(2)}, u32[]{:S(2)}) collective-permute-start(bf16[2,3,384,128]{3,2,1,0:T(8,128)(2,1)S(1)} %broadcast_select_fusion.3), channel_id=1, source_target_pairs={{0,2},{1,3},{2,0},{3,1},{4,6},{5,7},{6,4},{7,5},{8,10},{9,11},{10,... | collective-permute-start | bytes 1769480 | tf_op jit(solution)/shard_map/near_2/ppermute | solution.py:245
  63.8 32.6 %collective-permute-start.17 = (bf16[2,3,384,128]{3,2,1,0:T(8,128)(2,1)S(1)}, bf16[2,3,384,128]{3,2,1,0:T(8,128)(2,1)S(1)}, u32[]{:S(2)}, u32[]{:S(2)}) collective-permute-start(bf16[2,3,384,128]{3,2,1,0:T(8,128)(2,1)S(1)} %get-tuple-element.86.q_ref.q0_ref), channel_id=1, source_target_pairs={{4,0},{5,1},{6,2},{7,3},{8,4},{9,5},{10,6},{11,7},{12,8},{13,9},{1... | collective-permute-start | bytes 1769480 | tf_op jit(solution)/shard_map/far_4/ppermute | solution.py:245
  68.7 35.2 %collective-permute-start.9 = (bf16[2,1,192,128]{3,2,1,0:T(8,128)(2,1)S(1)}, bf16[2,1,192,128]{3,2,1,0:T(8,128)(2,1)S(1)}, u32[]{:S(2)}, u32[]{:S(2)}) collective-permute-start(bf16[2,1,192,128]{3,2,1,0:T(8,128)(2,1)S(1)} %get-tuple-element.71), channel_id=1, source_target_pairs={{0,1},{1,0},{2,3},{3,2},{4,5},{5,4},{6,7},{7,6},{8,9},{9,8},{10,11... | collective-permute-start | bytes 294920 | tf_op jit(solution)/shard_map/pair_out/ppermute | solution.py:245
  76.0 38.8 %collective-permute-start.19 = (bf16[2,2,384,128]{3,2,1,0:T(8,128)(2,1)S(1)}, bf16[2,2,384,128]{3,2,1,0:T(8,128)(2,1)S(1)}, u32[]{:S(2)}, u32[]{:S(2)}) collective-permute-start(bf16[2,2,384,128]{3,2,1,0:T(8,128)(2,1)S(1)} %get-tuple-element.89.q_ref.q0_ref), channel_id=1, source_target_pairs={{4,0},{5,1},{6,2},{7,3},{8,4},{9,5},{10,6},{11,7},{12,8},{13,9},{1... | collective-permute-start | bytes 1179656 | tf_op jit(solution)/shard_map/far_5/ppermute | solution.py:245
  96.4 18.9 %collective-permute-start.14 = (bf16[2,4,384,128]{3,2,1,0:T(8,128)(2,1)S(1)}, bf16[2,4,384,128]{3,2,1,0:T(8,128)(2,1)S(1)}, u32[]{:S(2)}, u32[]{:S(2)}) collective-permute-start(bf16[2,4,384,128]{3,2,1,0:T(8,128)(2,1)S(1)} %broadcast_select_fusion), channel_id=1, source_target_pairs={{0,2},{1,3},{2,0},{3,1},{4,6},{5,7},{6,4},{7,5},{8,10},{9,11},{10,... | collective-permute-start | bytes 2359304 | tf_op jit(solution)/shard_map/near_3/ppermute | solution.py:245
  96.6 7.7 %collective-permute-start.10 = (bf16[2,3,192,128]{3,2,1,0:T(8,128)(2,1)S(1)}, bf16[2,3,192,128]{3,2,1,0:T(8,128)(2,1)S(1)}, u32[]{:S(2)}, u32[]{:S(2)}) collective-permute-start(bf16[2,3,192,128]{3,2,1,0:T(8,128)(2,1)S(1)} %get-tuple-element.72), channel_id=1, source_target_pairs={{0,1},{1,0},{2,3},{3,2},{4,5},{5,4},{6,7},{7,6},{8,9},{9,8},{10,11... | collective-permute-start | bytes 884744 | tf_op jit(solution)/shard_map/pair_out/ppermute | solution.py:245
  103.7 7.2 %collective-permute-start.11 = (bf16[2,2,192,128]{3,2,1,0:T(8,128)(2,1)S(1)}, bf16[2,2,192,128]{3,2,1,0:T(8,128)(2,1)S(1)}, u32[]{:S(2)}, u32[]{:S(2)}) collective-permute-start(bf16[2,2,192,128]{3,2,1,0:T(8,128)(2,1)S(1)} %get-tuple-element.73), channel_id=1, source_target_pairs={{0,1},{1,0},{2,3},{3,2},{4,5},{5,4},{6,7},{7,6},{8,9},{9,8},{10,11... | collective-permute-start | bytes 589832 | tf_op jit(solution)/shard_map/pair_out/ppermute | solution.py:245
  103.9 2.0 %collective-permute-start.12 = (bf16[2,1,192,128]{3,2,1,0:T(8,128)(2,1)S(1)}, bf16[2,1,192,128]{3,2,1,0:T(8,128)(2,1)S(1)}, u32[]{:S(2)}, u32[]{:S(2)}) collective-permute-start(bf16[2,1,192,128]{3,2,1,0:T(8,128)(2,1)S(1)} %get-tuple-element.74), channel_id=1, source_target_pairs={{0,1},{1,0},{2,3},{3,2},{4,5},{5,4},{6,7},{7,6},{8,9},{9,8},{10,11... | collective-permute-start | bytes 294920 | tf_op jit(solution)/shard_map/pair_out/ppermute | solution.py:245
  104.3 12.3 %collective-permute-start.16 = (f32[10,2,384]{2,1,0:T(2,128)S(1)}, f32[10,2,384]{2,1,0:T(2,128)S(1)}, u32[]{:S(2)}, u32[]{:S(2)}) collective-permute-start(f32[10,2,384]{2,1,0:T(2,128)S(1)} %constant_dynamic-update-slice_fusion.st0_ref), channel_id=1, source_target_pairs={{4,0},{5,1},{6,2},{7,3},{8,4},{9,5},{10,6},{11,7},{12,8},{13,9},{1... | collective-permute-start | bytes 92168 | tf_op jit(solution)/shard_map/far_stats/ppermute | solution.py:245
  106.0 10.7 %collective-permute-start.15 = (f32[10,2,384]{2,1,0:T(2,128)S(1)}, f32[10,2,384]{2,1,0:T(2,128)S(1)}, u32[]{:S(2)}, u32[]{:S(2)}) collective-permute-start(f32[10,2,384]{2,1,0:T(2,128)S(1)} %constant_dynamic-update-slice_fusion.st0_ref), channel_id=1, source_target_pairs={{2,0},{3,1},{4,2},{5,3},{6,4},{7,5},{8,6},{9,7},{10,8},{11,9},{12,... | collective-permute-start | bytes 92168 | tf_op jit(solution)/shard_map/next_stats/ppermute | solution.py:245
  110.9 5.7 %collective-permute-start.21 = (bf16[2,1,384,128]{3,2,1,0:T(8,128)(2,1)S(1)}, bf16[2,1,384,128]{3,2,1,0:T(8,128)(2,1)S(1)}, u32[]{:S(2)}, u32[]{:S(2)}) collective-permute-start(bf16[2,1,384,128]{3,2,1,0:T(8,128)(2,1)S(1)} %get-tuple-element.92.q_ref.q0_ref), channel_id=1, source_target_pairs={{4,0},{5,1},{6,2},{7,3},{8,4},{9,5},{10,6},{11,7},{12,8},{13,9},{1... | collective-permute-start | bytes 589832 | tf_op jit(solution)/shard_map/far_6/ppermute | solution.py:245
  114.8 14.2 %collective-permute-start.18 = (bf16[2,3,384,128]{3,2,1,0:T(8,128)(2,1)S(1)}, bf16[2,3,384,128]{3,2,1,0:T(8,128)(2,1)S(1)}, u32[]{:S(2)}, u32[]{:S(2)}) collective-permute-start(bf16[2,3,384,128]{3,2,1,0:T(8,128)(2,1)S(1)} %broadcast_select_fusion.2), channel_id=1, source_target_pairs={{0,2},{1,3},{2,0},{3,1},{4,6},{5,7},{6,4},{7,5},{8,10},{9,11},{10,... | collective-permute-start | bytes 1769480 | tf_op jit(solution)/shard_map/near_4/ppermute | solution.py:245
  115.3 22.4 %collective-permute-start.20 = (bf16[2,2,384,128]{3,2,1,0:T(8,128)(2,1)S(1)}, bf16[2,2,384,128]{3,2,1,0:T(8,128)(2,1)S(1)}, u32[]{:S(2)}, u32[]{:S(2)}) collective-permute-start(bf16[2,2,384,128]{3,2,1,0:T(8,128)(2,1)S(1)} %broadcast_select_fusion.5), channel_id=1, source_target_pairs={{0,2},{1,3},{2,0},{3,1},{4,6},{5,7},{6,4},{7,5},{8,10},{9,11},{10,... | collective-permute-start | bytes 1179656 | tf_op jit(solution)/shard_map/near_5/ppermute | solution.py:245
  129.0 15.0 %collective-permute-start.22 = (bf16[2,1,384,128]{3,2,1,0:T(8,128)(2,1)S(1)}, bf16[2,1,384,128]{3,2,1,0:T(8,128)(2,1)S(1)}, u32[]{:S(2)}, u32[]{:S(2)}) collective-permute-start(bf16[2,1,384,128]{3,2,1,0:T(8,128)(2,1)S(1)} %broadcast_select_fusion.6), channel_id=1, source_target_pairs={{0,2},{1,3},{2,0},{3,1},{4,6},{5,7},{6,4},{7,5},{8,10},{9,11},{10,... | collective-permute-start | bytes 589832 | tf_op jit(solution)/shard_map/near_6/ppermute | solution.py:245
  134.4 12.1 %collective-permute-start.25 = (bf16[2,3,192,128]{3,2,1,0:T(8,128)(2,1)S(1)}, bf16[2,3,192,128]{3,2,1,0:T(8,128)(2,1)S(1)}, u32[]{:S(2)}, u32[]{:S(2)}) collective-permute-start(bf16[2,3,192,128]{3,2,1,0:T(8,128)(2,1)S(1)} %get-tuple-element.97), channel_id=1, source_target_pairs={{0,1},{1,0},{2,3},{3,2},{4,5},{5,4},{6,7},{7,6},{8,9},{9,8},{10,11... | collective-permute-start | bytes 884744 | tf_op jit(solution)/shard_map/pair_out/ppermute | solution.py:245
  137.6 8.9 %collective-permute-start.23 = (bf16[2,3,192,128]{3,2,1,0:T(8,128)(2,1)S(1)}, bf16[2,3,192,128]{3,2,1,0:T(8,128)(2,1)S(1)}, u32[]{:S(2)}, u32[]{:S(2)}) collective-permute-start(bf16[2,3,192,128]{3,2,1,0:T(8,128)(2,1)S(1)} %get-tuple-element.95), channel_id=1, source_target_pairs={{0,1},{1,0},{2,3},{3,2},{4,5},{5,4},{6,7},{7,6},{8,9},{9,8},{10,11... | collective-permute-start | bytes 884744 | tf_op jit(solution)/shard_map/pair_out/ppermute | solution.py:245
  141.3 6.2 %collective-permute-start.26 = (bf16[2,2,192,128]{3,2,1,0:T(8,128)(2,1)S(1)}, bf16[2,2,192,128]{3,2,1,0:T(8,128)(2,1)S(1)}, u32[]{:S(2)}, u32[]{:S(2)}) collective-permute-start(bf16[2,2,192,128]{3,2,1,0:T(8,128)(2,1)S(1)} %get-tuple-element.98), channel_id=1, source_target_pairs={{0,1},{1,0},{2,3},{3,2},{4,5},{5,4},{6,7},{7,6},{8,9},{9,8},{10,11... | collective-permute-start | bytes 589832 | tf_op jit(solution)/shard_map/pair_out/ppermute | solution.py:245
  143.9 2.6 %collective-permute-start.24 = (bf16[2,1,192,128]{3,2,1,0:T(8,128)(2,1)S(1)}, bf16[2,1,192,128]{3,2,1,0:T(8,128)(2,1)S(1)}, u32[]{:S(2)}, u32[]{:S(2)}) collective-permute-start(bf16[2,1,192,128]{3,2,1,0:T(8,128)(2,1)S(1)} %get-tuple-element.96), channel_id=1, source_target_pairs={{0,1},{1,0},{2,3},{3,2},{4,5},{5,4},{6,7},{7,6},{8,9},{9,8},{10,11... | collective-permute-start | bytes 294920 | tf_op jit(solution)/shard_map/pair_out/ppermute | solution.py:245
  146.0 1.4 collective-permute-start.27
  (8 other events, 17.4 us)

commit v2 on v1

v2 whole, which is shorter than its diff:
```python
import functools
import math

import jax
import jax.numpy as jnp
from jax import lax
from jax.experimental import pallas as pl
from jax.experimental.pallas import tpu as pltpu
from jax.sharding import PartitionSpec as P

FRAME = 64
AXES = ("ctx", "head")
GROUP = 4
MASKED = -1e30
CHUNKS = (2, 2, 1)
COST = 0.1
GATHER_BEFORE = 2
OVERLAP = True
VMEM = 16 * 2**20
SMALL = 8 * 2**20
NT = ((1,), (1,))
NN = ((1,), (0,))


def dot(a, b, dims):
    return lax.dot_general(a, b, (dims, ((), ())), preferred_element_type=jnp.float32)


def starts(sizes):
    return [sum(sizes[:i]) for i in range(len(sizes))]


def placed(done, side, core, keep_ref, theirs_ref, send_ref):
    rows = keep_ref.shape[2]
    mine = pl.multiple_of(core * rows, rows)
    other = pl.multiple_of((1 - core) * rows, rows)
    keep_ref[:, 0] = done[side, :, pl.ds(mine, rows), :]
    theirs_ref[:, 0] = done[side, :, pl.ds(other, rows), :]
    send_ref[:, 0] = done[1 - side]


def ordered(side, own_ref, beside_ref):
    first, second = [], []
    for i in range(2):
        own, beside = own_ref[i, 0], beside_ref[i, 0]
        first.append(jnp.where(side == 0, own, beside))
        second.append(jnp.where(side == 0, beside, own))
    return [tuple(first), tuple(second)]


def forward_kernel(
    where_ref, q_own, q_beside, kv_own, kv_beside, past_own, past_beside, cols_ref, docs_ref,
    keep_ref, theirs_ref, send_ref, stat_ref, done, *, scale
):
    span = q_own.shape[2]
    factor = scale * math.log2(math.e)
    side, core = where_ref[0], where_ref[1]
    queries = ordered(side, q_own, q_beside)
    blocks = ordered(side, past_own, past_beside) + ordered(side, kv_own, kv_beside)
    for part in range(2):
        query, grad = queries[part]
        at = part * span
        doc_col, limit_col = cols_ref[at : at + span, 0:1], cols_ref[at : at + span, 1:2]
        segments = blocks[part : part + 3]
        scores = []
        for i, (key, _) in enumerate(segments):
            raw = dot(query, key, NT) * factor
            allowed = docs_ref[:, at + i * span : at + (i + 1) * span] == doc_col
            if i == 2:
                place = at + lax.broadcasted_iota(jnp.int32, raw.shape, 1)
                allowed = allowed & (place <= limit_col)
            scores.append(jnp.where(allowed, raw, MASKED))
        top = functools.reduce(jnp.maximum, [jnp.max(s, axis=1, keepdims=True) for s in scores])
        raised = [jnp.exp2(s - top) for s in scores]
        total = functools.reduce(jnp.add, [jnp.sum(r, axis=1, keepdims=True) for r in raised])
        inverse = 1.0 / total
        probs = [r * inverse for r in raised]
        mixed = functools.reduce(
            jnp.add, [dot(p.astype(jnp.bfloat16), value, NN) for (_, value), p in zip(segments, probs)]
        )
        output = mixed.astype(jnp.bfloat16)
        delta = jnp.sum(grad.astype(jnp.float32) * output.astype(jnp.float32), axis=1, keepdims=True)
        grad_query = jnp.zeros_like(mixed)
        for (key, value), p in zip(segments, probs):
            grad_score = (p * (dot(grad, value, NT) - delta)).astype(jnp.bfloat16)
            grad_query += dot(grad_score, key, NN)
        done[part, 0] = output
        done[part, 1] = (grad_query * scale).astype(jnp.bfloat16)
        for i, column in enumerate((top + jnp.log2(total), delta)):
            stat_ref[0, i : i + 1, at : at + span] = jnp.broadcast_to(column, (span, 128)).T[0:1]
    placed(done, side, core, keep_ref, theirs_ref, send_ref)


def backward_kernel(
    where_ref, kv_own, kv_beside, q_own, q_beside, next_own, next_beside, stat_ref, next_stat_ref, cols_ref, rows_ref,
    keep_ref, theirs_ref, send_ref, done, *, scale
):
    span = kv_own.shape[2]
    factor = scale * math.log2(math.e)
    side, core = where_ref[0], where_ref[1]
    keys = ordered(side, kv_own, kv_beside)
    blocks = ordered(side, q_own, q_beside) + ordered(side, next_own, next_beside)
    for part in range(2):
        key, value = keys[part]
        at = part * span
        key_doc = cols_ref[at : at + span, 0:1]
        grad_key = jnp.zeros(key.shape, jnp.float32)
        grad_value = jnp.zeros(key.shape, jnp.float32)
        for i in range(3):
            query, grad = blocks[part + i]
            block = part + i
            lo = block * span
            stats = stat_ref if block < 2 else next_stat_ref
            here = (block % 2) * span
            raw = dot(key, query, NT) * factor
            allowed = key_doc == rows_ref[0:1, lo : lo + span]
            if i == 0:
                place = at + lax.broadcasted_iota(jnp.int32, raw.shape, 0)
                allowed = allowed & (place <= rows_ref[1:2, lo : lo + span])
            probs = jnp.exp2(jnp.where(allowed, raw - stats[0, 0:1, here : here + span], MASKED))
            grad_value += dot(probs.astype(jnp.bfloat16), grad, NN)
            grad_prob = dot(value, grad, NT)
            grad_score = (probs * (grad_prob - stats[0, 1:2, here : here + span])).astype(jnp.bfloat16)
            grad_key += dot(grad_score, query, NN)
        done[part, 0] = (grad_key * scale).astype(jnp.bfloat16)
        done[part, 1] = grad_value.astype(jnp.bfloat16)
    placed(done, side, core, keep_ref, theirs_ref, send_ref)


def per_head(shape, start=0):
    return pl.BlockSpec((shape[0], 1) + shape[2:], lambda h: (0, h + start, 0, 0))


def per_head_stats(shape, start=0):
    return pl.BlockSpec((1,) + shape[1:], lambda h: (h + start, 0, 0))


def whole(shape):
    return pl.BlockSpec(shape, lambda h: (0,) * len(shape))


def cost(heads, span, dim):
    pairs = heads * span * span * 3
    return pl.CostEstimate(
        flops=int(COST * 2 * pairs * dim * 4), bytes_accessed=int(COST * heads * span * dim * 2 * 10), transcendentals=int(COST * pairs)
    )


def attend(kernel, heads, here, arrays, stats, tables, scale, gives_stats):
    _, _, span, dim = arrays[0][0].shape
    rows = span // 2
    shapes = [(2, heads, rows, dim), (2, heads, rows, dim), (2, heads, span, dim)]
    out_specs = [per_head(shape) for shape in shapes]
    out_shape = [jax.ShapeDtypeStruct(shape, jnp.bfloat16) for shape in shapes]
    if gives_stats:
        out_specs.append(per_head_stats((heads, 2, 2 * span)))
        out_shape.append(jax.ShapeDtypeStruct((heads, 2, 2 * span), jnp.float32))
    return pl.pallas_call(
        functools.partial(kernel, scale=scale),
        grid=(heads,),
        in_specs=[pl.BlockSpec(memory_space=pltpu.SMEM)]
        + [per_head(x.shape, first) for x, first in arrays]
        + [per_head_stats(x.shape, first) for x, first in stats]
        + [whole(x.shape) for x in tables],
        out_specs=out_specs,
        out_shape=out_shape,
        scratch_shapes=[pltpu.VMEM((2, 2, span, dim), jnp.bfloat16)],
        compiler_params=pltpu.CompilerParams(vmem_limit_bytes=VMEM),
        cost_estimate=cost(2 * heads, span, dim),
    )(here, *[x for x, _ in arrays], *[x for x, _ in stats], *tables)


def finish(copies, sems):
    running = [pltpu.make_async_copy(a, b, sems.at[i]) for i, (a, b) in enumerate(copies)]
    for c in running:
        c.start()
    for c in running:
        c.wait()


def laid_out(where_ref, mine_ref, came_ref, own_ref, send_ref, staged, sems):
    side, core = where_ref[0], where_ref[1]
    half, rows = came_ref.shape[1], came_ref.shape[2]
    mine = pl.multiple_of(core * rows, rows)
    other = pl.multiple_of((1 - core) * rows, rows)
    finish(
        [(mine_ref, staged.at[:, :, pl.ds(mine, rows)]), (came_ref, staged.at[:, :, pl.ds(other, rows)])], sems
    )
    quarter = half // 2
    heads = [pl.ds(who * quarter, quarter) for who in (side, 1 - side)]
    finish([(staged.at[:, at], to) for at, to in zip(heads, (own_ref, send_ref))], sems)


def lay_out(here, mine, came):
    _, half, rows, dim = came.shape
    return pl.pallas_call(
        laid_out,
        in_specs=[pl.BlockSpec(memory_space=pltpu.SMEM)] + [pl.BlockSpec(memory_space=pl.ANY)] * 2,
        out_specs=[pl.BlockSpec(memory_space=pl.ANY)] * 2,
        out_shape=[jax.ShapeDtypeStruct((2, half // 2, 2 * rows, dim), came.dtype)] * 2,
        scratch_shapes=[pltpu.VMEM((2, half, 2 * rows, dim), came.dtype), pltpu.SemaphoreType.DMA((2,))],
        compiler_params=pltpu.CompilerParams(vmem_limit_bytes=SMALL),
        cost_estimate=pl.CostEstimate(flops=0, bytes_accessed=8 * half * rows * dim * 2, transcendentals=0),
    )(here, mine, came)


def gathered(where_ref, *refs, sizes):
    n = len(sizes)
    runs = [refs[4 * j : 4 * j + 4] for j in range(n)]
    results, sems = refs[4 * n : 4 * n + 2], refs[-1]
    side, core = where_ref[0], where_ref[1]
    quarter = sum(sizes)
    rows = results[0].shape[1]
    mine = pl.ds(pl.multiple_of(core * rows, rows), rows)
    copies = []
    for (begin, size), run in zip(zip(starts(sizes), sizes), runs):
        for k, ref in enumerate(run):
            which_core, which_side = (core, 1 - core)[k % 2], (side, 1 - side)[k // 2]
            at = pl.ds(which_core * 2 * quarter + which_side * quarter + begin, size)
            for i, to in enumerate(results):
                copies.append((ref.at[i, :, mine] if k >= 2 else ref.at[i], to.at[at]))
    finish(copies, sems)


def gather(here, runs):
    sizes = tuple(run[0].shape[1] for run in runs)
    _, _, rows, dim = runs[0][0].shape
    shape = (4 * sum(sizes), rows, dim)
    return pl.pallas_call(
        functools.partial(gathered, sizes=sizes),
        grid=(1,),
        in_specs=[pl.BlockSpec(memory_space=pltpu.SMEM)] + [whole(x.shape) for run in runs for x in run],
        out_specs=[pl.BlockSpec(memory_space=pl.ANY)] * 2,
        out_shape=[jax.ShapeDtypeStruct(shape, runs[0][0].dtype)] * 2,
        scratch_shapes=[pltpu.SemaphoreType.DMA((8 * len(sizes),))],
        compiler_params=pltpu.CompilerParams(vmem_limit_bytes=SMALL),
        cost_estimate=pl.CostEstimate(flops=0, bytes_accessed=16 * sum(sizes) * rows * dim * 2, transcendentals=0),
    )(here, *[x for run in runs for x in run])


def tied(x, *after):
    return lax.optimization_barrier((x,) + after)[0] if after else x


def local(query_in, key_in, value_in, grad_out, doc_ids, frame_kind):
    rows_own, heads, dim = query_in.shape
    half = heads // 2
    span = 2 * rows_own
    count = lax.axis_size("ctx") * lax.axis_size("head")
    at = lax.axis_index("ctx") * lax.axis_size("head") + lax.axis_index("head")
    core = at % 2
    side = (at // 2) % 2
    base = (at - at % GROUP) * rows_own
    scale = dim**-0.5
    here = jnp.stack([side, core]).astype(jnp.int32)

    def sent(x, pairs, name):
        with jax.named_scope(name):
            return lax.ppermute(x, AXES, [(i, j) for i, j in pairs if 0 <= j < count])

    ahead = [(i, i + GROUP) for i in range(count)]
    behind = [(i, i - GROUP) for i in range(count)]
    across = [(i, i ^ 1) for i in range(count)]
    beside = [(i, i ^ 2) for i in range(count)]

    by_head = [x.transpose(1, 0, 2) for x in (key_in, value_in, query_in, grad_out)]

    def halves(x, y, which):
        return jnp.stack([lax.dynamic_slice_in_dim(a, which * half, half, 0) for a in (x, y)])

    quarter = half // 2
    cuts = tuple(zip(starts(CHUNKS), CHUNKS))
    came_kv = sent(halves(*by_head[:2], 1 - core), across, "pair_kv")
    kv_own, kv_send = lay_out(here, halves(*by_head[:2], core), came_kv)
    past_own = sent(kv_own, ahead, "far_kv_own")
    kv_beside = sent(kv_send, beside, "side_kv")
    came_q = sent(tied(halves(*by_head[2:], 1 - core), came_kv), across, "pair_q")
    q_own, q_send = lay_out(here, halves(*by_head[2:], core), came_q)
    past_beside = sent(tied(kv_beside, q_own, past_own), ahead, "far_kv_beside")
    q_beside = sent(tied(q_send, kv_beside), beside, "side_q")

    doc_ids, frame_kind = tied((doc_ids, frame_kind), came_q)
    reach = GROUP * rows_own
    docs = jnp.concatenate(
        [jnp.full((reach,), -1, jnp.int32), doc_ids, jnp.full((reach,), -2, jnp.int32)]
    )
    docs = lax.dynamic_slice_in_dim(docs, base, 3 * reach)
    kinds = lax.dynamic_slice_in_dim(frame_kind, base // FRAME, reach // FRAME)
    place = jnp.arange(reach, dtype=jnp.int32)
    limit = jnp.where(jnp.repeat(kinds, FRAME) == 1, (place // FRAME) * FRAME + FRAME - 1, place)
    rows = jnp.stack([docs[reach:], jnp.concatenate([limit, limit])])
    cols = rows[:, :reach].T
    key_docs = docs[None, : 2 * reach]

    pieces, coming = [], []
    for start, size in cuts:
        pick = slice(start, start + size)
        both = jnp.concatenate([q_own[:, pick], q_beside[:, pick]], axis=1)
        pieces.append(both)

    def returned(keep, theirs, came, name, *after):
        return keep, sent(tied(theirs, *after), across, "pair_" + name), came, sent(tied(came, *after), across, "pair_of_" + name)

    arrays = [(x, 0) for x in (q_own, q_beside, kv_own, kv_beside, past_own, past_beside)]
    *found, stats = attend(forward_kernel, quarter, here, arrays, [], [cols, key_docs], scale, True)
    out_came = sent(found[2], beside, "side_out")
    runs = []
    next_stats = None
    for j, (start, size) in enumerate(cuts):
        after = [next_stats] if j else [past_beside]
        if j >= 2:
            after.append(runs[0][0])
        coming.append(sent(tied(pieces[j], *after), behind, f"far_q_{start}"))
        if j == 0:
            next_stats = sent(tied(stats, coming[0]), behind, "far_stats")
        x = coming[j]
        arrays = [(a, start) for a in (kv_own, kv_beside, q_own, q_beside)] + [(x, 0), (x, size)]
        at = tied(here, results[0]) if j == GATHER_BEFORE else here
        grads = attend(
            backward_kernel, size, at, arrays, [(stats, start), (next_stats, start)], [cols, rows], scale, False
        )
        if j == 0:
            results = list(gather(tied(here, grads[0]), [returned(*found[:2], out_came, "out", grads[0])]))
        came = sent(grads[2], beside, f"side_grads_{start}")
        runs.append(returned(*grads[:2], came, f"grads_{start}"))
    results += list(gather(here, runs))
    return tuple(x.transpose(1, 0, 2) for x in results)


def solution(mesh):
    placed = P(AXES, None, None)
    return jax.shard_map(
        local,
        mesh=mesh,
        in_specs=(placed,) * 4 + (P(), P()),
        out_specs=(placed,) * 4,
        check_vma=False,
    )
```

time: 151 us -> 136 us (0.901)
  starting transfers between devices: 53.1 us -> 27.2 us
  waiting for transfers between devices: 34.6 us -> 55.5 us
  Pallas kernels: 49.9 us -> 41.5 us
  other arithmetic: 5.53 us -> 2.66 us
  local copies, waits for them, and re-layouts: 5.15 us -> 7.38 us
    ppermute x28 -> x22, starting transfers between devices: 53.1 us -> 27.2 us  [sent(): return lax.ppermute(x, AXES, [(i, j) for i, j in pairs if 0 <= j < count])]
    ppermute x28 -> x22, waiting for transfers between devices: 34.6 us -> 55.5 us  [sent(): return lax.ppermute(x, AXES, [(i, j) for i, j in pairs if 0 <= j < count])]
    pallas_call x10 -> x4, Pallas kernels: 40.9 us -> 34.7 us  [attend(): pl.pallas_call(functools.partial(kernel, scale=scale), grid=(heads,), in_...]
    select_n x7 -> x0, other arithmetic: 3.19 us -> none  [local(): jnp.where(side == 0, first, second)]
    pallas_call x4, Pallas kernels: 8.94 us -> 6.77 us  [the longest x2 3.88 us: gather(): pl.pallas_call(functools.partial(gathered, sizes=sizes), grid=(1,), in_sp...]
    unnamed x28 -> x18, local copies, waits for them, and re-layouts: 3.5 us -> 3.56 us
  transfers between devices with their start and end apart: 28 -> 22, of which waited for: 7 -> 11; matrix products, arithmetic and copies ran while one was open for 3% -> 3% of each run, Pallas kernels for 30% -> 29%
where the time goes in v2:
time: 136 us; the launch traced here: 135 us
  waiting for transfers between devices  55.5 us (41%)
  Pallas kernels  41.5 us (31%)
  starting transfers between devices  27.2 us (20%)
  local copies, waits for them, and re-layouts  7.38 us (5%)
  other arithmetic  2.66 us (2%)
    ppermute x22, waiting for transfers between devices, sent(): return lax.ppermute(x, AXES, [(i, j) for i, j in pairs if 0 <= j < count])  55.5 us
    pallas_call x4, Pallas kernels, attend(): pl.pallas_call(functools.partial(kernel, scale=scale), grid=(heads,), in_...  34.7 us
    ppermute x22, starting transfers between devices, sent(): return lax.ppermute(x, AXES, [(i, j) for i, j in pairs if 0 <= j < count])  27.2 us
    pallas_call x2, Pallas kernels, gather(): pl.pallas_call(functools.partial(gathered, sizes=sizes), grid=(1,), in_sp...  3.88 us
    unnamed x18, local copies, waits for them, and re-layouts  3.56 us
    pallas_call x2, Pallas kernels, lay_out(): pl.pallas_call(laid_out, in_specs=[pl.BlockSpec(memory_space=pltpu.SMEM)]...  2.89 us
  transfers between devices with their start and end apart: 22, of which 11 were waited for; matrix products, arithmetic and copies ran while one was open for 3% of the time, Pallas kernels for 29%

profile of v2, /device:TPU:27, one launch (start us, length us, event | category | flops | bytes accessed | tf_op | source)
XLA Modules:
  0.0 135.3 jit_solution(3828699622468793116)
XLA Ops:
  0.7 1.6 %dynamic-slice_bitcast_fusion.4 = (bf16[1,10,192,128]{3,2,1,0:T(8,128)(2,1)S(1)}, bf16[1,10,192,128]{3,2,1,0:T(8,128)(2,1)S(1)}, bf16[1,10,192,128]{3,2,1,0:T(8,128)(2,1)S(1)}, bf16[1,10,192,128]{3,2,1,0:T(8,128)(2,1)S(1)}) fusion(bf16[192,20,128]{2,0,1:T(8,128)(2,1)} %param.8, s32[]{:T(128)S(6)} %select_n.52, s32[]{:T(128)S(6)} %select_n.51, ...), kind=kLoop, calls=%fused_computation.10 | loop fusion | bytes 3932168 | tf_op jit(solution)/shard_map/stack | solution.py:269
  2.3 1.0 pad_maximum_fusion.1
  4.2 1.1 copy-done.5
  6.8 1.1 shard_map.93
  7.9 1.3 collective-permute-start.1
  9.2 1.3 collective-permute-start.4
  10.6 1.8 %shard_map.94 = (bf16[2,5,384,128]{3,2,1,0:T(8,128)(2,1)S(1)}, bf16[2,5,384,128]{3,2,1,0:T(8,128)(2,1)}) custom-call(s32[2]{0:T(128)S(1)} %pad_add_fusion.2.where_ref, bf16[2,10,192,128]{3,2,1,0:T(8,128)(2,1)S(1)} %pad_maximum_fusion.2.mine_ref, bf16[2,10,192,128]{3,2,1,0:T(8,128)(2,1)S(1)} %collective-permute-done.2.came_ref), custom_call_target="tpu_custom_call" | custom-call | bytes 3932160 | tf_op jit(solution)/shard_map/pallas_call | solution.py:196
  12.4 18.8 %collective-permute-done.1.kv_beside = bf16[2,5,384,128]{3,2,1,0:T(8,128)(2,1)S(1)} collective-permute-done((bf16[2,5,384,128]{3,2,1,0:T(8,128)(2,1)S(1)}, bf16[2,5,384,128]{3,2,1,0:T(8,128)(2,1)S(1)}, u32[]{:S(2)}, u32[]{:S(2)}) %collective-permute-start.1) | collective-permute-done | bytes 983072 | tf_op jit(solution)/shard_map/side_kv/ppermute | solution.py:259
  32.2 1.2 collective-permute-start.3
  34.1 1.3 collective-permute-start.5
  36.5 18.4 %collective-permute-done.3.q_beside = bf16[2,5,384,128]{3,2,1,0:T(8,128)(2,1)S(1)} collective-permute-done((bf16[2,5,384,128]{3,2,1,0:T(8,128)(2,1)}, bf16[2,5,384,128]{3,2,1,0:T(8,128)(2,1)S(1)}, u32[]{:S(2)}, u32[]{:S(2)}) %collective-permute-start.3) | collective-permute-done | bytes 983072 | tf_op jit(solution)/shard_map/side_q/ppermute | solution.py:259
  55.7 0.9 pad_maximum_fusion.4
  56.7 1.5 %collective-permute-done.5.past_beside = bf16[2,5,384,128]{3,2,1,0:T(8,128)(2,1)} collective-permute-done((bf16[2,5,384,128]{3,2,1,0:T(8,128)(2,1)}, bf16[2,5,384,128]{3,2,1,0:T(8,128)(2,1)}, u32[]{:S(2)}, u32[]{:S(2)}) %collective-permute-start.5) | collective-permute-done | bytes 983072 | tf_op jit(solution)/shard_map/far_kv_beside/ppermute | solution.py:259
  58.2 4.8 %collective-permute-start.6 = (bf16[2,4,384,128]{3,2,1,0:T(8,128)(2,1)}, bf16[2,4,384,128]{3,2,1,0:T(8,128)(2,1)}, u32[]{:S(2)}, u32[]{:S(2)}) collective-permute-start(bf16[2,4,384,128]{3,2,1,0:T(8,128)(2,1)} %pad_maximum_fusion.4), channel_id=1, source_target_pairs={{4,0},{5,1},{6,2},{7,3},{8,4},{9,5},{10,6},{11,7},{12,8},{13,9},{1... | collective-permute-start | bytes 2359304 | tf_op jit(solution)/shard_map/far_q_0/ppermute | solution.py:259
  63.3 1.2 copy-done.1
  64.5 18.4 %shard_map.95 = (bf16[2,5,192,128]{3,2,1,0:T(8,128)(2,1)S(1)}, bf16[2,5,192,128]{3,2,1,0:T(8,128)(2,1)S(1)}, bf16[2,5,384,128]{3,2,1,0:T(8,128)(2,1)S(1)}, f32[5,2,768]{2,1,0:T(2,128)S(1)}) custom-call(s32[2]{0:T(128)S(1)} %pad_add_fusion.2.where_ref, bf16[2,5,384,128]{3,2,1,0:T(8,128)(2,1)S(1)} %get-tuple-element.41.q_own, ...), custom_call_target="tpu_custom_call" | custom-call | flops 452984832 | bytes 983040 | tf_op jit(solution)/shard_map/pallas_call | solution.py:158
  83.3 1.3 collective-permute-start.7
  85.6 3.7 %collective-permute-start.14 = (bf16[2,4,384,128]{3,2,1,0:T(8,128)(2,1)S(1)}, bf16[2,4,384,128]{3,2,1,0:T(8,128)(2,1)S(1)}, u32[]{:S(2)}, u32[]{:S(2)}) collective-permute-start(bf16[2,4,384,128]{3,2,1,0:T(8,128)(2,1)S(1)} %pad_maximum_fusion.5), channel_id=1, source_target_pairs={{4,0},{5,1},{6,2},{7,3},{8,4},{9,5},{10,6},{11,7},{12,8},{13,9},{1... | collective-permute-start | bytes 2359304 | tf_op jit(solution)/shard_map/far_q_2/ppermute | solution.py:259
  89.3 6.7 %shard_map.96 = (bf16[2,2,192,128]{3,2,1,0:T(8,128)(2,1)S(1)}, bf16[2,2,192,128]{3,2,1,0:T(8,128)(2,1)S(1)}, bf16[2,2,384,128]{3,2,1,0:T(8,128)(2,1)S(1)}) custom-call(s32[2]{0:T(128)S(1)} %pad_add_fusion.2.where_ref, bf16[2,5,384,128]{3,2,1,0:T(8,128)(2,1)S(1)} %get-tuple-element.38.kv_own, bf16[2,5,384,128]{3,2,1,0:T(8,128)(2,1)S(1)} %copy-done.2, ...), custom_call_target="tpu_custom_call" | custom-call | flops 181193936 | bytes 393216 | tf_op jit(solution)/shard_map/pallas_call | solution.py:158
  96.0 7.8 %collective-permute-done.9.refs_2_ = bf16[2,5,384,128]{3,2,1,0:T(8,128)(2,1)S(1)} collective-permute-done((bf16[2,5,384,128]{3,2,1,0:T(8,128)(2,1)S(1)}, bf16[2,5,384,128]{3,2,1,0:T(8,128)(2,1)S(1)}, u32[]{:S(2)}, u32[]{:S(2)}) %collective-permute-start.9) | collective-permute-done | bytes 983072 | tf_op jit(solution)/shard_map/side_out/ppermute | solution.py:259
  103.8 3.4 %collective-permute-start.10 = (bf16[2,5,384,128]{3,2,1,0:T(8,128)(2,1)S(1)}, bf16[2,5,384,128]{3,2,1,0:T(8,128)(2,1)S(1)}, u32[]{:S(2)}, u32[]{:S(2)}) collective-permute-start(bf16[2,5,384,128]{3,2,1,0:T(8,128)(2,1)S(1)} %collective-permute-done.9.refs_2_), channel_id=1, source_target_pairs={{0,1},{1,0},{2,3},{3,2},{4,5},{5,4},{6,7},{7,6},{8,9},{9,8},{10,11... | collective-permute-start | bytes 2949128 | tf_op jit(solution)/shard_map/pair_of_out/ppermute | solution.py:259
  107.7 1.5 %collective-permute-start.18 = (bf16[2,2,384,128]{3,2,1,0:T(8,128)(2,1)S(1)}, bf16[2,2,384,128]{3,2,1,0:T(8,128)(2,1)S(1)}, u32[]{:S(2)}, u32[]{:S(2)}) collective-permute-start(bf16[2,2,384,128]{3,2,1,0:T(8,128)(2,1)S(1)} %pad_maximum_fusion.6), channel_id=1, source_target_pairs={{4,0},{5,1},{6,2},{7,3},{8,4},{9,5},{10,6},{11,7},{12,8},{13,9},{1... | collective-permute-start | bytes 1179656 | tf_op jit(solution)/shard_map/far_q_4/ppermute | solution.py:259
  109.2 6.3 %shard_map.98 = (bf16[2,2,192,128]{3,2,1,0:T(8,128)(2,1)S(1)}, bf16[2,2,192,128]{3,2,1,0:T(8,128)(2,1)S(1)}, bf16[2,2,384,128]{3,2,1,0:T(8,128)(2,1)S(1)}) custom-call(s32[2]{0:T(128)S(1)} %pad_add_fusion.2.where_ref, bf16[2,5,384,128]{3,2,1,0:T(8,128)(2,1)S(1)} %get-tuple-element.38.kv_own, bf16[2,5,384,128]{3,2,1,0:T(8,128)(2,1)S(1)} %copy-done.2, ...), custom_call_target="tpu_custom_call" | custom-call | flops 181193936 | bytes 393216 | tf_op jit(solution)/shard_map/pallas_call | solution.py:158
  115.5 1.3 collective-permute-start.16
  117.7 1.6 %collective-permute-start.13 = (bf16[2,2,384,128]{3,2,1,0:T(8,128)(2,1)S(1)}, bf16[2,2,384,128]{3,2,1,0:T(8,128)(2,1)S(1)}, u32[]{:S(2)}, u32[]{:S(2)}) collective-permute-start(bf16[2,2,384,128]{3,2,1,0:T(8,128)(2,1)S(1)} %collective-permute-done.12.refs_2_), channel_id=1, source_target_pairs={{0,1},{1,0},{2,3},{3,2},{4,5},{5,4},{6,7},{7,6},{8,9},{9,8},{10,11... | collective-permute-start | bytes 1179656 | tf_op jit(solution)/shard_map/pair_of_grads_0/ppermute | solution.py:259
  119.3 1.9 %shard_map.97 = (bf16[20,192,128]{2,1,0:T(8,128)(2,1)}, bf16[20,192,128]{2,1,0:T(8,128)(2,1)}) custom-call(s32[2]{0:T(128)S(1)} %pad_add_fusion.2.where_ref, bf16[2,5,192,128]{3,2,1,0:T(8,128)(2,1)S(1)} %get-tuple-element.52.refs_0_, bf16[2,5,192,128]{3,2,1,0:T(8,128)(2,1)S(1)} %collective-permute-done.8.refs_1_, ...), custom_call_target="tpu_custom_call" | custom-call | bytes 3932160 | tf_op jit(solution)/shard_map/pallas_call | solution.py:229
  121.2 3.3 %shard_map.99 = (bf16[2,1,192,128]{3,2,1,0:T(8,128)(2,1)S(1)}, bf16[2,1,192,128]{3,2,1,0:T(8,128)(2,1)S(1)}, bf16[2,1,384,128]{3,2,1,0:T(8,128)(2,1)S(1)}) custom-call(s32[2]{0:T(128)S(1)} %pad_add_fusion.2.where_ref, bf16[2,5,384,128]{3,2,1,0:T(8,128)(2,1)S(1)} %get-tuple-element.38.kv_own, bf16[2,5,384,128]{3,2,1,0:T(8,128)(2,1)S(1)} %copy-done.2, ...), custom_call_target="tpu_custom_call" | custom-call | flops 90596968 | bytes 196608 | tf_op jit(solution)/shard_map/pallas_call | solution.py:158
  124.6 1.5 %collective-permute-done.16.refs_6_ = bf16[2,2,384,128]{3,2,1,0:T(8,128)(2,1)S(1)} collective-permute-done((bf16[2,2,384,128]{3,2,1,0:T(8,128)(2,1)S(1)}, bf16[2,2,384,128]{3,2,1,0:T(8,128)(2,1)S(1)}, u32[]{:S(2)}, u32[]{:S(2)}) %collective-permute-start.16) | collective-permute-done | bytes 393248 | tf_op jit(solution)/shard_map/side_grads_2/ppermute | solution.py:259
  126.1 1.3 collective-permute-start.17
  127.9 3.1 %collective-permute-done.20.refs_10_ = bf16[2,1,384,128]{3,2,1,0:T(8,128)(2,1)S(1)} collective-permute-done((bf16[2,1,384,128]{3,2,1,0:T(8,128)(2,1)S(1)}, bf16[2,1,384,128]{3,2,1,0:T(8,128)(2,1)S(1)}, u32[]{:S(2)}, u32[]{:S(2)}) %collective-permute-start.20) | collective-permute-done | bytes 196640 | tf_op jit(solution)/shard_map/side_grads_4/ppermute | solution.py:259
  131.9 1.3 collective-permute-done.19.refs_9_
  133.2 2.0 %shard_map.100 = (bf16[20,192,128]{2,1,0:T(8,128)(2,1)}, bf16[20,192,128]{2,1,0:T(8,128)(2,1)}) custom-call(s32[2]{0:T(128)S(1)} %pad_add_fusion.2.where_ref, bf16[2,2,192,128]{3,2,1,0:T(8,128)(2,1)S(1)} %get-tuple-element.50.refs_0_, bf16[2,2,192,128]{3,2,1,0:T(8,128)(2,1)S(1)} %collective-permute-done.11.refs_1_, ...), custom_call_target="tpu_custom_call" | custom-call | bytes 3932160 | tf_op jit(solution)/shard_map/pallas_call | solution.py:229
  (67 shorter events, 10.2 us)
Async XLA Ops:
  3.3 3.1 %collective-permute-start = (bf16[2,10,192,128]{3,2,1,0:T(8,128)(2,1)}, bf16[2,10,192,128]{3,2,1,0:T(8,128)(2,1)S(1)}, u32[]{:S(2)}, u32[]{:S(2)}) collective-permute-start(bf16[2,10,192,128]{3,2,1,0:T(8,128)(2,1)} %pad_maximum_fusion.1), channel_id=1, source_target_pairs={{0,1},{1,0},{2,3},{3,2},{4,5},{5,4},{6,7},{7,6},{8,9},{9,8},{10,11... | collective-permute-start | bytes 2949128 | tf_op jit(solution)/shard_map/pair_kv/ppermute | solution.py:259
  4.1 1.2 copy-start.5
  4.1 1.5 %copy-start.6 = (bf16[192,20,128]{2,0,1:T(8,128)(2,1)S(1)}, bf16[192,20,128]{2,0,1:T(8,128)(2,1)}, u32[]{:S(2)}) copy-start(bf16[192,20,128]{2,0,1:T(8,128)(2,1)} %param.6) | copy-start | bytes 2949124
  6.4 4.1 %collective-permute-start.2 = (bf16[2,10,192,128]{3,2,1,0:T(8,128)(2,1)S(1)}, bf16[2,10,192,128]{3,2,1,0:T(8,128)(2,1)S(1)}, u32[]{:S(2)}, u32[]{:S(2)}) collective-permute-start(bf16[2,10,192,128]{3,2,1,0:T(8,128)(2,1)S(1)} %pad_maximum_fusion.3), channel_id=1, source_target_pairs={{0,1},{1,0},{2,3},{3,2},{4,5},{5,4},{6,7},{7,6},{8,9},{9,8},{10,11... | collective-permute-start | bytes 2949128 | tf_op jit(solution)/shard_map/pair_q/ppermute | solution.py:259
  7.9 23.4 %collective-permute-start.1 = (bf16[2,5,384,128]{3,2,1,0:T(8,128)(2,1)S(1)}, bf16[2,5,384,128]{3,2,1,0:T(8,128)(2,1)S(1)}, u32[]{:S(2)}, u32[]{:S(2)}) collective-permute-start(bf16[2,5,384,128]{3,2,1,0:T(8,128)(2,1)S(1)} %get-tuple-element.39), channel_id=1, source_target_pairs={{0,2},{1,3},{2,0},{3,1},{4,6},{5,7},{6,4},{7,5},{8,10},{9,11},{10,... | collective-permute-start | bytes 2949128 | tf_op jit(solution)/shard_map/side_kv/ppermute | solution.py:259
  9.2 24.9 %collective-permute-start.4 = (bf16[2,5,384,128]{3,2,1,0:T(8,128)(2,1)S(1)}, bf16[2,5,384,128]{3,2,1,0:T(8,128)(2,1)}, u32[]{:S(2)}, u32[]{:S(2)}) collective-permute-start(bf16[2,5,384,128]{3,2,1,0:T(8,128)(2,1)S(1)} %get-tuple-element.38.kv_own), channel_id=1, source_target_pairs={{0,4},{1,5},{2,6},{3,7},{4,8},{5,9},{6,10},{7,11},{8,12},{9,13},{1... | collective-permute-start | bytes 2949128 | tf_op jit(solution)/shard_map/far_kv_own/ppermute | solution.py:259
  31.3 0.9 copy-start
  32.2 22.7 %collective-permute-start.3 = (bf16[2,5,384,128]{3,2,1,0:T(8,128)(2,1)}, bf16[2,5,384,128]{3,2,1,0:T(8,128)(2,1)S(1)}, u32[]{:S(2)}, u32[]{:S(2)}) collective-permute-start(bf16[2,5,384,128]{3,2,1,0:T(8,128)(2,1)} %get-tuple-element.43), channel_id=1, source_target_pairs={{0,2},{1,3},{2,0},{3,1},{4,6},{5,7},{6,4},{7,5},{8,10},{9,11},{10,... | collective-permute-start | bytes 2949128 | tf_op jit(solution)/shard_map/side_q/ppermute | solution.py:259
  33.4 2.2 %copy-start.7 = (s32[6144]{0:T(1024)S(1)}, s32[6144]{0:T(1024)}, u32[]{:S(2)}) copy-start(s32[6144]{0:T(1024)} %param.10) | copy-start | bytes 73732
  33.4 1.9 %copy-start.8 = (s32[96]{0:T(128)S(1)}, s32[96]{0:T(128)}, u32[]{:S(2)}) copy-start(s32[96]{0:T(128)} %param.11) | copy-start | bytes 1156
  34.1 24.2 %collective-permute-start.5 = (bf16[2,5,384,128]{3,2,1,0:T(8,128)(2,1)}, bf16[2,5,384,128]{3,2,1,0:T(8,128)(2,1)}, u32[]{:S(2)}, u32[]{:S(2)}) collective-permute-start(bf16[2,5,384,128]{3,2,1,0:T(8,128)(2,1)} %copy-done), channel_id=1, source_target_pairs={{0,4},{1,5},{2,6},{3,7},{4,8},{5,9},{6,10},{7,11},{8,12},{9,13},{1... | collective-permute-start | bytes 2949128 | tf_op jit(solution)/shard_map/far_kv_beside/ppermute | solution.py:259
  58.2 25.1 %collective-permute-start.6 = (bf16[2,4,384,128]{3,2,1,0:T(8,128)(2,1)}, bf16[2,4,384,128]{3,2,1,0:T(8,128)(2,1)}, u32[]{:S(2)}, u32[]{:S(2)}) collective-permute-start(bf16[2,4,384,128]{3,2,1,0:T(8,128)(2,1)} %pad_maximum_fusion.4), channel_id=1, source_target_pairs={{4,0},{5,1},{6,2},{7,3},{8,4},{9,5},{10,6},{11,7},{12,8},{13,9},{1... | collective-permute-start | bytes 2359304 | tf_op jit(solution)/shard_map/far_q_0/ppermute | solution.py:259
  63.3 1.2 copy-start.1
  64.5 20.1 %copy-start.3 = (bf16[2,2,384,128]{3,2,1,0:T(8,128)(2,1)S(1)}, bf16[2,2,384,128]{3,2,1,0:T(8,128)(2,1)}, u32[]{:S(2)}) copy-start(bf16[2,2,384,128]{3,2,1,0:T(8,128)(2,1)} %get-tuple-element.72) | copy-start | bytes 1179652
  64.5 20.1 %copy-start.4 = (bf16[2,2,384,128]{3,2,1,0:T(8,128)(2,1)S(1)}, bf16[2,2,384,128]{3,2,1,0:T(8,128)(2,1)}, u32[]{:S(2)}) copy-start(bf16[2,2,384,128]{3,2,1,0:T(8,128)(2,1)} %get-tuple-element.74) | copy-start | bytes 1179652
  83.0 6.3 %copy-start.2 = (bf16[2,5,384,128]{3,2,1,0:T(8,128)(2,1)S(1)}, bf16[2,5,384,128]{3,2,1,0:T(8,128)(2,1)}, u32[]{:S(2)}) copy-start(bf16[2,5,384,128]{3,2,1,0:T(8,128)(2,1)} %copy-done) | copy-start | bytes 2949124
  83.0 20.8 %collective-permute-start.9 = (bf16[2,5,384,128]{3,2,1,0:T(8,128)(2,1)S(1)}, bf16[2,5,384,128]{3,2,1,0:T(8,128)(2,1)S(1)}, u32[]{:S(2)}, u32[]{:S(2)}) collective-permute-start(bf16[2,5,384,128]{3,2,1,0:T(8,128)(2,1)S(1)} %get-tuple-element.55), channel_id=1, source_target_pairs={{0,2},{1,3},{2,0},{3,1},{4,6},{5,7},{6,4},{7,5},{8,10},{9,11},{10,... | collective-permute-start | bytes 2949128 | tf_op jit(solution)/shard_map/side_out/ppermute | solution.py:259
  83.3 2.3 %collective-permute-start.7 = (f32[5,2,768]{2,1,0:T(2,128)S(1)}, f32[5,2,768]{2,1,0:T(2,128)S(1)}, u32[]{:S(2)}, u32[]{:S(2)}) collective-permute-start(f32[5,2,768]{2,1,0:T(2,128)S(1)} %get-tuple-element.49.stat_ref), channel_id=1, source_target_pairs={{4,0},{5,1},{6,2},{7,3},{8,4},{9,5},{10,6},{11,7},{12,8},{13,9},{1... | collective-permute-start | bytes 92168 | tf_op jit(solution)/shard_map/far_stats/ppermute | solution.py:259
  85.6 23.6 %collective-permute-start.14 = (bf16[2,4,384,128]{3,2,1,0:T(8,128)(2,1)S(1)}, bf16[2,4,384,128]{3,2,1,0:T(8,128)(2,1)S(1)}, u32[]{:S(2)}, u32[]{:S(2)}) collective-permute-start(bf16[2,4,384,128]{3,2,1,0:T(8,128)(2,1)S(1)} %pad_maximum_fusion.5), channel_id=1, source_target_pairs={{4,0},{5,1},{6,2},{7,3},{8,4},{9,5},{10,6},{11,7},{12,8},{13,9},{1... | collective-permute-start | bytes 2359304 | tf_op jit(solution)/shard_map/far_q_2/ppermute | solution.py:259
  103.8 15.5 %collective-permute-start.10 = (bf16[2,5,384,128]{3,2,1,0:T(8,128)(2,1)S(1)}, bf16[2,5,384,128]{3,2,1,0:T(8,128)(2,1)S(1)}, u32[]{:S(2)}, u32[]{:S(2)}) collective-permute-start(bf16[2,5,384,128]{3,2,1,0:T(8,128)(2,1)S(1)} %collective-permute-done.9.refs_2_), channel_id=1, source_target_pairs={{0,1},{1,0},{2,3},{3,2},{4,5},{5,4},{6,7},{7,6},{8,9},{9,8},{10,11... | collective-permute-start | bytes 2949128 | tf_op jit(solution)/shard_map/pair_of_out/ppermute | solution.py:259
  107.3 12.0 %collective-permute-start.8 = (bf16[2,5,192,128]{3,2,1,0:T(8,128)(2,1)S(1)}, bf16[2,5,192,128]{3,2,1,0:T(8,128)(2,1)S(1)}, u32[]{:S(2)}, u32[]{:S(2)}) collective-permute-start(bf16[2,5,192,128]{3,2,1,0:T(8,128)(2,1)S(1)} %get-tuple-element.54), channel_id=1, source_target_pairs={{0,1},{1,0},{2,3},{3,2},{4,5},{5,4},{6,7},{7,6},{8,9},{9,8},{10,11... | collective-permute-start | bytes 1474568 | tf_op jit(solution)/shard_map/pair_out/ppermute | solution.py:259
  107.4 10.3 %collective-permute-start.12 = (bf16[2,2,384,128]{3,2,1,0:T(8,128)(2,1)S(1)}, bf16[2,2,384,128]{3,2,1,0:T(8,128)(2,1)S(1)}, u32[]{:S(2)}, u32[]{:S(2)}) collective-permute-start(bf16[2,2,384,128]{3,2,1,0:T(8,128)(2,1)S(1)} %get-tuple-element.60), channel_id=1, source_target_pairs={{0,2},{1,3},{2,0},{3,1},{4,6},{5,7},{6,4},{7,5},{8,10},{9,11},{10,... | collective-permute-start | bytes 1179656 | tf_op jit(solution)/shard_map/side_grads_0/ppermute | solution.py:259
  107.7 13.5 %collective-permute-start.18 = (bf16[2,2,384,128]{3,2,1,0:T(8,128)(2,1)S(1)}, bf16[2,2,384,128]{3,2,1,0:T(8,128)(2,1)S(1)}, u32[]{:S(2)}, u32[]{:S(2)}) collective-permute-start(bf16[2,2,384,128]{3,2,1,0:T(8,128)(2,1)S(1)} %pad_maximum_fusion.6), channel_id=1, source_target_pairs={{4,0},{5,1},{6,2},{7,3},{8,4},{9,5},{10,6},{11,7},{12,8},{13,9},{1... | collective-permute-start | bytes 1179656 | tf_op jit(solution)/shard_map/far_q_4/ppermute | solution.py:259
  115.5 10.6 %collective-permute-start.16 = (bf16[2,2,384,128]{3,2,1,0:T(8,128)(2,1)S(1)}, bf16[2,2,384,128]{3,2,1,0:T(8,128)(2,1)S(1)}, u32[]{:S(2)}, u32[]{:S(2)}) collective-permute-start(bf16[2,2,384,128]{3,2,1,0:T(8,128)(2,1)S(1)} %get-tuple-element.64), channel_id=1, source_target_pairs={{0,2},{1,3},{2,0},{3,1},{4,6},{5,7},{6,4},{7,5},{8,10},{9,11},{10,... | collective-permute-start | bytes 1179656 | tf_op jit(solution)/shard_map/side_grads_2/ppermute | solution.py:259
  117.7 14.2 %collective-permute-start.13 = (bf16[2,2,384,128]{3,2,1,0:T(8,128)(2,1)S(1)}, bf16[2,2,384,128]{3,2,1,0:T(8,128)(2,1)S(1)}, u32[]{:S(2)}, u32[]{:S(2)}) collective-permute-start(bf16[2,2,384,128]{3,2,1,0:T(8,128)(2,1)S(1)} %collective-permute-done.12.refs_2_), channel_id=1, source_target_pairs={{0,1},{1,0},{2,3},{3,2},{4,5},{5,4},{6,7},{7,6},{8,9},{9,8},{10,11... | collective-permute-start | bytes 1179656 | tf_op jit(solution)/shard_map/pair_of_grads_0/ppermute | solution.py:259
  124.5 6.6 %collective-permute-start.20 = (bf16[2,1,384,128]{3,2,1,0:T(8,128)(2,1)S(1)}, bf16[2,1,384,128]{3,2,1,0:T(8,128)(2,1)S(1)}, u32[]{:S(2)}, u32[]{:S(2)}) collective-permute-start(bf16[2,1,384,128]{3,2,1,0:T(8,128)(2,1)S(1)} %get-tuple-element.69), channel_id=1, source_target_pairs={{0,2},{1,3},{2,0},{3,1},{4,6},{5,7},{6,4},{7,5},{8,10},{9,11},{10,... | collective-permute-start | bytes 589832 | tf_op jit(solution)/shard_map/side_grads_4/ppermute | solution.py:259
  126.1 7.1 %collective-permute-start.17 = (bf16[2,2,384,128]{3,2,1,0:T(8,128)(2,1)S(1)}, bf16[2,2,384,128]{3,2,1,0:T(8,128)(2,1)S(1)}, u32[]{:S(2)}, u32[]{:S(2)}) collective-permute-start(bf16[2,2,384,128]{3,2,1,0:T(8,128)(2,1)S(1)} %collective-permute-done.16.refs_6_), channel_id=1, source_target_pairs={{0,1},{1,0},{2,3},{3,2},{4,5},{5,4},{6,7},{7,6},{8,9},{9,8},{10,11... | collective-permute-start | bytes 1179656 | tf_op jit(solution)/shard_map/pair_of_grads_2/ppermute | solution.py:259
  127.4 4.4 %collective-permute-start.11 = (bf16[2,2,192,128]{3,2,1,0:T(8,128)(2,1)S(1)}, bf16[2,2,192,128]{3,2,1,0:T(8,128)(2,1)S(1)}, u32[]{:S(2)}, u32[]{:S(2)}) collective-permute-start(bf16[2,2,192,128]{3,2,1,0:T(8,128)(2,1)S(1)} %get-tuple-element.59), channel_id=1, source_target_pairs={{0,1},{1,0},{2,3},{3,2},{4,5},{5,4},{6,7},{7,6},{8,9},{9,8},{10,11... | collective-permute-start | bytes 589832 | tf_op jit(solution)/shard_map/pair_grads_0/ppermute | solution.py:259
  127.4 4.5 %collective-permute-start.15 = (bf16[2,2,192,128]{3,2,1,0:T(8,128)(2,1)S(1)}, bf16[2,2,192,128]{3,2,1,0:T(8,128)(2,1)S(1)}, u32[]{:S(2)}, u32[]{:S(2)}) collective-permute-start(bf16[2,2,192,128]{3,2,1,0:T(8,128)(2,1)S(1)} %get-tuple-element.63), channel_id=1, source_target_pairs={{0,1},{1,0},{2,3},{3,2},{4,5},{5,4},{6,7},{7,6},{8,9},{9,8},{10,11... | collective-permute-start | bytes 589832 | tf_op jit(solution)/shard_map/pair_grads_2/ppermute | solution.py:259
  131.1 2.1 %collective-permute-start.21 = (bf16[2,1,384,128]{3,2,1,0:T(8,128)(2,1)S(1)}, bf16[2,1,384,128]{3,2,1,0:T(8,128)(2,1)S(1)}, u32[]{:S(2)}, u32[]{:S(2)}) collective-permute-start(bf16[2,1,384,128]{3,2,1,0:T(8,128)(2,1)S(1)} %collective-permute-done.20.refs_10_), channel_id=1, source_target_pairs={{0,1},{1,0},{2,3},{3,2},{4,5},{5,4},{6,7},{7,6},{8,9},{9,8},{10,11... | collective-permute-start | bytes 589832 | tf_op jit(solution)/shard_map/pair_of_grads_4/ppermute | solution.py:259
  131.9 1.3 collective-permute-start.19

commit v3 on v2

--- a/solution.py
+++ b/solution.py
@@ -15,7 +15,6 @@
 CHUNKS = (2, 2, 1)
 COST = 0.1
 GATHER_BEFORE = 2
-OVERLAP = True
 VMEM = 16 * 2**20
 SMALL = 8 * 2**20
 NT = ((1,), (1,))
@@ -274,9 +273,10 @@
     kv_own, kv_send = lay_out(here, halves(*by_head[:2], core), came_kv)
     past_own = sent(kv_own, ahead, "far_kv_own")
     kv_beside = sent(kv_send, beside, "side_kv")
-    came_q = sent(tied(halves(*by_head[2:], 1 - core), came_kv), across, "pair_q")
-    q_own, q_send = lay_out(here, halves(*by_head[2:], core), came_q)
-    past_beside = sent(tied(kv_beside, q_own, past_own), ahead, "far_kv_beside")
+    q_in, g_in = tied(tuple(by_head[2:]), kv_own)
+    came_q = sent(halves(q_in, g_in, 1 - core), across, "pair_q")
+    q_own, q_send = lay_out(here, halves(q_in, g_in, core), came_q)
+    past_beside = sent(tied(kv_beside, past_own), ahead, "far_kv_beside")
     q_beside = sent(tied(q_send, kv_beside), beside, "side_q")
 
     doc_ids, frame_kind = tied((doc_ids, frame_kind), came_q)

time: 136 us -> 135 us (level)
  local copies, waits for them, and re-layouts: 7.38 us -> 5.86 us
  waiting for transfers between devices: 55.5 us -> 57 us
    ppermute x22, waiting for transfers between devices: 55.5 us -> 57 us  [sent(): return lax.ppermute(x, AXES, [(i, j) for i, j in pairs if 0 <= j < count])]
    unnamed x18 -> x20, local copies, waits for them, and re-layouts: 3.56 us -> 2.33 us
where the time goes in v3:
time: 135 us; the launch traced here: 134 us
  waiting for transfers between devices  57 us (42%)
  Pallas kernels  41.5 us (31%)
  starting transfers between devices  27.2 us (20%)
  local copies, waits for them, and re-layouts  5.86 us (4%)
  other arithmetic  1.72 us (1%)
    ppermute x22, waiting for transfers between devices, sent(): return lax.ppermute(x, AXES, [(i, j) for i, j in pairs if 0 <= j < count])  57 us
    pallas_call x4, Pallas kernels, attend(): pl.pallas_call(functools.partial(kernel, scale=scale), grid=(heads,), in_...  34.7 us
    ppermute x22, starting transfers between devices, sent(): return lax.ppermute(x, AXES, [(i, j) for i, j in pairs if 0 <= j < count])  27.2 us
    pallas_call x2, Pallas kernels, gather(): pl.pallas_call(functools.partial(gathered, sizes=sizes), grid=(1,), in_sp...  3.88 us
    pallas_call x2, Pallas kernels, lay_out(): pl.pallas_call(laid_out, in_specs=[pl.BlockSpec(memory_space=pltpu.SMEM)]...  2.89 us
  transfers between devices with their start and end apart: 22, of which 11 were waited for; matrix products, arithmetic and copies ran while one was open for 3% of the time, Pallas kernels for 29%

profile of v3, /device:TPU:27, one launch (start us, length us, event | category | flops | bytes accessed | tf_op | source)
XLA Modules:
  0.0 134.4 jit_solution(6694755353174412565)
XLA Ops:
  0.7 1.3 dynamic-slice_bitcast_fusion.4
  3.3 2.0 %collective-permute-done.came_ref = bf16[2,10,192,128]{3,2,1,0:T(8,128)(2,1)S(1)} collective-permute-done((bf16[2,10,192,128]{3,2,1,0:T(8,128)(2,1)S(1)}, bf16[2,10,192,128]{3,2,1,0:T(8,128)(2,1)S(1)}, u32[]{:S(2)}, u32[]{:S(2)}) %collective-permute-start) | collective-permute-done | bytes 983072 | tf_op jit(solution)/shard_map/pair_kv/ppermute | solution.py:258
  5.3 1.1 shard_map.93
  7.0 1.2 collective-permute-start.1
  8.3 1.3 collective-permute-start.4
  9.7 1.8 %shard_map.94 = (bf16[2,5,384,128]{3,2,1,0:T(8,128)(2,1)S(1)}, bf16[2,5,384,128]{3,2,1,0:T(8,128)(2,1)}) custom-call(s32[2]{0:T(128)S(1)} %pad_add_fusion.2.where_ref, bf16[2,10,192,128]{3,2,1,0:T(8,128)(2,1)S(1)} %pad_maximum_fusion.2.mine_ref, bf16[2,10,192,128]{3,2,1,0:T(8,128)(2,1)S(1)} %collective-permute-done.2.came_ref), custom_call_target="tpu_custom_call" | custom-call | bytes 3932160 | tf_op jit(solution)/shard_map/pallas_call | solution.py:195
  11.5 18.8 %collective-permute-done.1.kv_beside = bf16[2,5,384,128]{3,2,1,0:T(8,128)(2,1)S(1)} collective-permute-done((bf16[2,5,384,128]{3,2,1,0:T(8,128)(2,1)S(1)}, bf16[2,5,384,128]{3,2,1,0:T(8,128)(2,1)S(1)}, u32[]{:S(2)}, u32[]{:S(2)}) %collective-permute-start.1) | collective-permute-done | bytes 983072 | tf_op jit(solution)/shard_map/side_kv/ppermute | solution.py:258
  30.4 0.9 copy-done
  31.3 1.2 collective-permute-start.3
  33.2 1.3 collective-permute-start.5
  35.6 18.4 %collective-permute-done.3.q_beside = bf16[2,5,384,128]{3,2,1,0:T(8,128)(2,1)S(1)} collective-permute-done((bf16[2,5,384,128]{3,2,1,0:T(8,128)(2,1)}, bf16[2,5,384,128]{3,2,1,0:T(8,128)(2,1)S(1)}, u32[]{:S(2)}, u32[]{:S(2)}) %collective-permute-start.3) | collective-permute-done | bytes 983072 | tf_op jit(solution)/shard_map/side_q/ppermute | solution.py:258
  54.8 0.9 pad_maximum_fusion.4
  55.8 1.5 %collective-permute-done.5.past_beside = bf16[2,5,384,128]{3,2,1,0:T(8,128)(2,1)} collective-permute-done((bf16[2,5,384,128]{3,2,1,0:T(8,128)(2,1)}, bf16[2,5,384,128]{3,2,1,0:T(8,128)(2,1)}, u32[]{:S(2)}, u32[]{:S(2)}) %collective-permute-start.5) | collective-permute-done | bytes 983072 | tf_op jit(solution)/shard_map/far_kv_beside/ppermute | solution.py:258
  57.3 4.8 %collective-permute-start.6 = (bf16[2,4,384,128]{3,2,1,0:T(8,128)(2,1)}, bf16[2,4,384,128]{3,2,1,0:T(8,128)(2,1)}, u32[]{:S(2)}, u32[]{:S(2)}) collective-permute-start(bf16[2,4,384,128]{3,2,1,0:T(8,128)(2,1)} %pad_maximum_fusion.4), channel_id=1, source_target_pairs={{4,0},{5,1},{6,2},{7,3},{8,4},{9,5},{10,6},{11,7},{12,8},{13,9},{1... | collective-permute-start | bytes 2359304 | tf_op jit(solution)/shard_map/far_q_0/ppermute | solution.py:258
  62.4 1.2 copy-done.1
  63.6 18.4 %shard_map.95 = (bf16[2,5,192,128]{3,2,1,0:T(8,128)(2,1)S(1)}, bf16[2,5,192,128]{3,2,1,0:T(8,128)(2,1)S(1)}, bf16[2,5,384,128]{3,2,1,0:T(8,128)(2,1)S(1)}, f32[5,2,768]{2,1,0:T(2,128)S(1)}) custom-call(s32[2]{0:T(128)S(1)} %pad_add_fusion.2.where_ref, bf16[2,5,384,128]{3,2,1,0:T(8,128)(2,1)S(1)} %get-tuple-element.43.q_own, ...), custom_call_target="tpu_custom_call" | custom-call | flops 452984832 | bytes 983040 | tf_op jit(solution)/shard_map/pallas_call | solution.py:157
  82.4 1.3 collective-permute-start.7
  84.7 3.7 %collective-permute-start.14 = (bf16[2,4,384,128]{3,2,1,0:T(8,128)(2,1)S(1)}, bf16[2,4,384,128]{3,2,1,0:T(8,128)(2,1)S(1)}, u32[]{:S(2)}, u32[]{:S(2)}) collective-permute-start(bf16[2,4,384,128]{3,2,1,0:T(8,128)(2,1)S(1)} %pad_maximum_fusion.5), channel_id=1, source_target_pairs={{4,0},{5,1},{6,2},{7,3},{8,4},{9,5},{10,6},{11,7},{12,8},{13,9},{1... | collective-permute-start | bytes 2359304 | tf_op jit(solution)/shard_map/far_q_2/ppermute | solution.py:258
  88.4 6.7 %shard_map.96 = (bf16[2,2,192,128]{3,2,1,0:T(8,128)(2,1)S(1)}, bf16[2,2,192,128]{3,2,1,0:T(8,128)(2,1)S(1)}, bf16[2,2,384,128]{3,2,1,0:T(8,128)(2,1)S(1)}) custom-call(s32[2]{0:T(128)S(1)} %pad_add_fusion.2.where_ref, bf16[2,5,384,128]{3,2,1,0:T(8,128)(2,1)S(1)} %get-tuple-element.39.kv_own, bf16[2,5,384,128]{3,2,1,0:T(8,128)(2,1)S(1)} %copy-done.2, ...), custom_call_target="tpu_custom_call" | custom-call | flops 181193936 | bytes 393216 | tf_op jit(solution)/shard_map/pallas_call | solution.py:157
  95.1 7.8 %collective-permute-done.9.refs_2_ = bf16[2,5,384,128]{3,2,1,0:T(8,128)(2,1)S(1)} collective-permute-done((bf16[2,5,384,128]{3,2,1,0:T(8,128)(2,1)S(1)}, bf16[2,5,384,128]{3,2,1,0:T(8,128)(2,1)S(1)}, u32[]{:S(2)}, u32[]{:S(2)}) %collective-permute-start.9) | collective-permute-done | bytes 983072 | tf_op jit(solution)/shard_map/side_out/ppermute | solution.py:258
  102.9 3.4 %collective-permute-start.10 = (bf16[2,5,384,128]{3,2,1,0:T(8,128)(2,1)S(1)}, bf16[2,5,384,128]{3,2,1,0:T(8,128)(2,1)S(1)}, u32[]{:S(2)}, u32[]{:S(2)}) collective-permute-start(bf16[2,5,384,128]{3,2,1,0:T(8,128)(2,1)S(1)} %collective-permute-done.9.refs_2_), channel_id=1, source_target_pairs={{0,1},{1,0},{2,3},{3,2},{4,5},{5,4},{6,7},{7,6},{8,9},{9,8},{10,11... | collective-permute-start | bytes 2949128 | tf_op jit(solution)/shard_map/pair_of_out/ppermute | solution.py:258
  106.8 1.5 %collective-permute-start.18 = (bf16[2,2,384,128]{3,2,1,0:T(8,128)(2,1)S(1)}, bf16[2,2,384,128]{3,2,1,0:T(8,128)(2,1)S(1)}, u32[]{:S(2)}, u32[]{:S(2)}) collective-permute-start(bf16[2,2,384,128]{3,2,1,0:T(8,128)(2,1)S(1)} %pad_maximum_fusion.6), channel_id=1, source_target_pairs={{4,0},{5,1},{6,2},{7,3},{8,4},{9,5},{10,6},{11,7},{12,8},{13,9},{1... | collective-permute-start | bytes 1179656 | tf_op jit(solution)/shard_map/far_q_4/ppermute | solution.py:258
  108.3 6.3 %shard_map.98 = (bf16[2,2,192,128]{3,2,1,0:T(8,128)(2,1)S(1)}, bf16[2,2,192,128]{3,2,1,0:T(8,128)(2,1)S(1)}, bf16[2,2,384,128]{3,2,1,0:T(8,128)(2,1)S(1)}) custom-call(s32[2]{0:T(128)S(1)} %pad_add_fusion.2.where_ref, bf16[2,5,384,128]{3,2,1,0:T(8,128)(2,1)S(1)} %get-tuple-element.39.kv_own, bf16[2,5,384,128]{3,2,1,0:T(8,128)(2,1)S(1)} %copy-done.2, ...), custom_call_target="tpu_custom_call" | custom-call | flops 181193936 | bytes 393216 | tf_op jit(solution)/shard_map/pallas_call | solution.py:157
  114.6 1.3 collective-permute-start.16
  116.8 1.6 %collective-permute-start.13 = (bf16[2,2,384,128]{3,2,1,0:T(8,128)(2,1)S(1)}, bf16[2,2,384,128]{3,2,1,0:T(8,128)(2,1)S(1)}, u32[]{:S(2)}, u32[]{:S(2)}) collective-permute-start(bf16[2,2,384,128]{3,2,1,0:T(8,128)(2,1)S(1)} %collective-permute-done.12.refs_2_), channel_id=1, source_target_pairs={{0,1},{1,0},{2,3},{3,2},{4,5},{5,4},{6,7},{7,6},{8,9},{9,8},{10,11... | collective-permute-start | bytes 1179656 | tf_op jit(solution)/shard_map/pair_of_grads_0/ppermute | solution.py:258
  118.4 1.9 %shard_map.97 = (bf16[20,192,128]{2,1,0:T(8,128)(2,1)}, bf16[20,192,128]{2,1,0:T(8,128)(2,1)}) custom-call(s32[2]{0:T(128)S(1)} %pad_add_fusion.2.where_ref, bf16[2,5,192,128]{3,2,1,0:T(8,128)(2,1)S(1)} %get-tuple-element.54.refs_0_, bf16[2,5,192,128]{3,2,1,0:T(8,128)(2,1)S(1)} %collective-permute-done.8.refs_1_, ...), custom_call_target="tpu_custom_call" | custom-call | bytes 3932160 | tf_op jit(solution)/shard_map/pallas_call | solution.py:228
  120.3 3.3 %shard_map.99 = (bf16[2,1,192,128]{3,2,1,0:T(8,128)(2,1)S(1)}, bf16[2,1,192,128]{3,2,1,0:T(8,128)(2,1)S(1)}, bf16[2,1,384,128]{3,2,1,0:T(8,128)(2,1)S(1)}) custom-call(s32[2]{0:T(128)S(1)} %pad_add_fusion.2.where_ref, bf16[2,5,384,128]{3,2,1,0:T(8,128)(2,1)S(1)} %get-tuple-element.39.kv_own, bf16[2,5,384,128]{3,2,1,0:T(8,128)(2,1)S(1)} %copy-done.2, ...), custom_call_target="tpu_custom_call" | custom-call | flops 90596968 | bytes 196608 | tf_op jit(solution)/shard_map/pallas_call | solution.py:157
  123.7 1.5 %collective-permute-done.16.refs_6_ = bf16[2,2,384,128]{3,2,1,0:T(8,128)(2,1)S(1)} collective-permute-done((bf16[2,2,384,128]{3,2,1,0:T(8,128)(2,1)S(1)}, bf16[2,2,384,128]{3,2,1,0:T(8,128)(2,1)S(1)}, u32[]{:S(2)}, u32[]{:S(2)}) %collective-permute-start.16) | collective-permute-done | bytes 393248 | tf_op jit(solution)/shard_map/side_grads_2/ppermute | solution.py:258
  125.2 1.3 collective-permute-start.17
  127.0 3.1 %collective-permute-done.20.refs_10_ = bf16[2,1,384,128]{3,2,1,0:T(8,128)(2,1)S(1)} collective-permute-done((bf16[2,1,384,128]{3,2,1,0:T(8,128)(2,1)S(1)}, bf16[2,1,384,128]{3,2,1,0:T(8,128)(2,1)S(1)}, u32[]{:S(2)}, u32[]{:S(2)}) %collective-permute-start.20) | collective-permute-done | bytes 196640 | tf_op jit(solution)/shard_map/side_grads_4/ppermute | solution.py:258
  131.0 1.3 collective-permute-done.19.refs_9_
  132.3 2.0 %shard_map.100 = (bf16[20,192,128]{2,1,0:T(8,128)(2,1)}, bf16[20,192,128]{2,1,0:T(8,128)(2,1)}) custom-call(s32[2]{0:T(128)S(1)} %pad_add_fusion.2.where_ref, bf16[2,2,192,128]{3,2,1,0:T(8,128)(2,1)S(1)} %get-tuple-element.52.refs_0_, bf16[2,2,192,128]{3,2,1,0:T(8,128)(2,1)S(1)} %collective-permute-done.11.refs_1_, ...), custom_call_target="tpu_custom_call" | custom-call | bytes 3932160 | tf_op jit(solution)/shard_map/pallas_call | solution.py:228
  (70 shorter events, 8.8 us)
Async XLA Ops:
  0.7 1.5 %copy-start.5 = (bf16[192,20,128]{2,0,1:T(8,128)(2,1)S(1)}, bf16[192,20,128]{2,0,1:T(8,128)(2,1)}, u32[]{:S(2)}) copy-start(bf16[192,20,128]{2,0,1:T(8,128)(2,1)} %param.7) | copy-start | bytes 2949124
  2.3 2.9 %collective-permute-start = (bf16[2,10,192,128]{3,2,1,0:T(8,128)(2,1)S(1)}, bf16[2,10,192,128]{3,2,1,0:T(8,128)(2,1)S(1)}, u32[]{:S(2)}, u32[]{:S(2)}) collective-permute-start(bf16[2,10,192,128]{3,2,1,0:T(8,128)(2,1)S(1)} %pad_maximum_fusion.1), channel_id=1, source_target_pairs={{0,1},{1,0},{2,3},{3,2},{4,5},{5,4},{6,7},{7,6},{8,9},{9,8},{10,11... | collective-permute-start | bytes 2949128 | tf_op jit(solution)/shard_map/pair_kv/ppermute | solution.py:258
  3.2 3.1 %copy-start.6 = (bf16[192,20,128]{2,0,1:T(8,128)(2,1)S(1)}, bf16[192,20,128]{2,0,1:T(8,128)(2,1)}, u32[]{:S(2)}) copy-start(bf16[192,20,128]{2,0,1:T(8,128)(2,1)} %param.9) | copy-start | bytes 2949124
  3.3 3.1 %copy-start.7 = (bf16[192,20,128]{2,0,1:T(8,128)(2,1)S(1)}, bf16[192,20,128]{2,0,1:T(8,128)(2,1)}, u32[]{:S(2)}) copy-start(bf16[192,20,128]{2,0,1:T(8,128)(2,1)} %param.6) | copy-start | bytes 2949124
  6.6 3.1 %collective-permute-start.2 = (bf16[2,10,192,128]{3,2,1,0:T(8,128)(2,1)S(1)}, bf16[2,10,192,128]{3,2,1,0:T(8,128)(2,1)S(1)}, u32[]{:S(2)}, u32[]{:S(2)}) collective-permute-start(bf16[2,10,192,128]{3,2,1,0:T(8,128)(2,1)S(1)} %pad_maximum_fusion.3), channel_id=1, source_target_pairs={{0,1},{1,0},{2,3},{3,2},{4,5},{5,4},{6,7},{7,6},{8,9},{9,8},{10,11... | collective-permute-start | bytes 2949128 | tf_op jit(solution)/shard_map/pair_q/ppermute | solution.py:258
  7.0 23.3 %collective-permute-start.1 = (bf16[2,5,384,128]{3,2,1,0:T(8,128)(2,1)S(1)}, bf16[2,5,384,128]{3,2,1,0:T(8,128)(2,1)S(1)}, u32[]{:S(2)}, u32[]{:S(2)}) collective-permute-start(bf16[2,5,384,128]{3,2,1,0:T(8,128)(2,1)S(1)} %get-tuple-element.40), channel_id=1, source_target_pairs={{0,2},{1,3},{2,0},{3,1},{4,6},{5,7},{6,4},{7,5},{8,10},{9,11},{10,... | collective-permute-start | bytes 2949128 | tf_op jit(solution)/shard_map/side_kv/ppermute | solution.py:258
  8.3 24.9 %collective-permute-start.4 = (bf16[2,5,384,128]{3,2,1,0:T(8,128)(2,1)S(1)}, bf16[2,5,384,128]{3,2,1,0:T(8,128)(2,1)}, u32[]{:S(2)}, u32[]{:S(2)}) collective-permute-start(bf16[2,5,384,128]{3,2,1,0:T(8,128)(2,1)S(1)} %get-tuple-element.39.kv_own), channel_id=1, source_target_pairs={{0,4},{1,5},{2,6},{3,7},{4,8},{5,9},{6,10},{7,11},{8,12},{9,13},{1... | collective-permute-start | bytes 2949128 | tf_op jit(solution)/shard_map/far_kv_own/ppermute | solution.py:258
  30.4 0.9 copy-start
  31.3 22.7 %collective-permute-start.3 = (bf16[2,5,384,128]{3,2,1,0:T(8,128)(2,1)}, bf16[2,5,384,128]{3,2,1,0:T(8,128)(2,1)S(1)}, u32[]{:S(2)}, u32[]{:S(2)}) collective-permute-start(bf16[2,5,384,128]{3,2,1,0:T(8,128)(2,1)} %get-tuple-element.45), channel_id=1, source_target_pairs={{0,2},{1,3},{2,0},{3,1},{4,6},{5,7},{6,4},{7,5},{8,10},{9,11},{10,... | collective-permute-start | bytes 2949128 | tf_op jit(solution)/shard_map/side_q/ppermute | solution.py:258
  32.5 2.2 %copy-start.8 = (s32[6144]{0:T(1024)S(1)}, s32[6144]{0:T(1024)}, u32[]{:S(2)}) copy-start(s32[6144]{0:T(1024)} %param.10) | copy-start | bytes 73732
  32.5 1.9 %copy-start.9 = (s32[96]{0:T(128)S(1)}, s32[96]{0:T(128)}, u32[]{:S(2)}) copy-start(s32[96]{0:T(128)} %param.11) | copy-start | bytes 1156
  33.2 24.2 %collective-permute-start.5 = (bf16[2,5,384,128]{3,2,1,0:T(8,128)(2,1)}, bf16[2,5,384,128]{3,2,1,0:T(8,128)(2,1)}, u32[]{:S(2)}, u32[]{:S(2)}) collective-permute-start(bf16[2,5,384,128]{3,2,1,0:T(8,128)(2,1)} %copy-done), channel_id=1, source_target_pairs={{0,4},{1,5},{2,6},{3,7},{4,8},{5,9},{6,10},{7,11},{8,12},{9,13},{1... | collective-permute-start | bytes 2949128 | tf_op jit(solution)/shard_map/far_kv_beside/ppermute | solution.py:258
  57.3 25.1 %collective-permute-start.6 = (bf16[2,4,384,128]{3,2,1,0:T(8,128)(2,1)}, bf16[2,4,384,128]{3,2,1,0:T(8,128)(2,1)}, u32[]{:S(2)}, u32[]{:S(2)}) collective-permute-start(bf16[2,4,384,128]{3,2,1,0:T(8,128)(2,1)} %pad_maximum_fusion.4), channel_id=1, source_target_pairs={{4,0},{5,1},{6,2},{7,3},{8,4},{9,5},{10,6},{11,7},{12,8},{13,9},{1... | collective-permute-start | bytes 2359304 | tf_op jit(solution)/shard_map/far_q_0/ppermute | solution.py:258
  62.4 1.2 copy-start.1
  63.6 20.0 %copy-start.3 = (bf16[2,2,384,128]{3,2,1,0:T(8,128)(2,1)S(1)}, bf16[2,2,384,128]{3,2,1,0:T(8,128)(2,1)}, u32[]{:S(2)}) copy-start(bf16[2,2,384,128]{3,2,1,0:T(8,128)(2,1)} %get-tuple-element.74) | copy-start | bytes 1179652
  63.6 20.1 %copy-start.4 = (bf16[2,2,384,128]{3,2,1,0:T(8,128)(2,1)S(1)}, bf16[2,2,384,128]{3,2,1,0:T(8,128)(2,1)}, u32[]{:S(2)}) copy-start(bf16[2,2,384,128]{3,2,1,0:T(8,128)(2,1)} %get-tuple-element.76) | copy-start | bytes 1179652
  82.1 6.3 %copy-start.2 = (bf16[2,5,384,128]{3,2,1,0:T(8,128)(2,1)S(1)}, bf16[2,5,384,128]{3,2,1,0:T(8,128)(2,1)}, u32[]{:S(2)}) copy-start(bf16[2,5,384,128]{3,2,1,0:T(8,128)(2,1)} %copy-done) | copy-start | bytes 2949124
  82.1 20.8 %collective-permute-start.9 = (bf16[2,5,384,128]{3,2,1,0:T(8,128)(2,1)S(1)}, bf16[2,5,384,128]{3,2,1,0:T(8,128)(2,1)S(1)}, u32[]{:S(2)}, u32[]{:S(2)}) collective-permute-start(bf16[2,5,384,128]{3,2,1,0:T(8,128)(2,1)S(1)} %get-tuple-element.57), channel_id=1, source_target_pairs={{0,2},{1,3},{2,0},{3,1},{4,6},{5,7},{6,4},{7,5},{8,10},{9,11},{10,... | collective-permute-start | bytes 2949128 | tf_op jit(solution)/shard_map/side_out/ppermute | solution.py:258
  82.4 2.3 %collective-permute-start.7 = (f32[5,2,768]{2,1,0:T(2,128)S(1)}, f32[5,2,768]{2,1,0:T(2,128)S(1)}, u32[]{:S(2)}, u32[]{:S(2)}) collective-permute-start(f32[5,2,768]{2,1,0:T(2,128)S(1)} %get-tuple-element.51.stat_ref), channel_id=1, source_target_pairs={{4,0},{5,1},{6,2},{7,3},{8,4},{9,5},{10,6},{11,7},{12,8},{13,9},{1... | collective-permute-start | bytes 92168 | tf_op jit(solution)/shard_map/far_stats/ppermute | solution.py:258
  84.7 23.6 %collective-permute-start.14 = (bf16[2,4,384,128]{3,2,1,0:T(8,128)(2,1)S(1)}, bf16[2,4,384,128]{3,2,1,0:T(8,128)(2,1)S(1)}, u32[]{:S(2)}, u32[]{:S(2)}) collective-permute-start(bf16[2,4,384,128]{3,2,1,0:T(8,128)(2,1)S(1)} %pad_maximum_fusion.5), channel_id=1, source_target_pairs={{4,0},{5,1},{6,2},{7,3},{8,4},{9,5},{10,6},{11,7},{12,8},{13,9},{1... | collective-permute-start | bytes 2359304 | tf_op jit(solution)/shard_map/far_q_2/ppermute | solution.py:258
  102.9 15.5 %collective-permute-start.10 = (bf16[2,5,384,128]{3,2,1,0:T(8,128)(2,1)S(1)}, bf16[2,5,384,128]{3,2,1,0:T(8,128)(2,1)S(1)}, u32[]{:S(2)}, u32[]{:S(2)}) collective-permute-start(bf16[2,5,384,128]{3,2,1,0:T(8,128)(2,1)S(1)} %collective-permute-done.9.refs_2_), channel_id=1, source_target_pairs={{0,1},{1,0},{2,3},{3,2},{4,5},{5,4},{6,7},{7,6},{8,9},{9,8},{10,11... | collective-permute-start | bytes 2949128 | tf_op jit(solution)/shard_map/pair_of_out/ppermute | solution.py:258
  106.4 12.0 %collective-permute-start.8 = (bf16[2,5,192,128]{3,2,1,0:T(8,128)(2,1)S(1)}, bf16[2,5,192,128]{3,2,1,0:T(8,128)(2,1)S(1)}, u32[]{:S(2)}, u32[]{:S(2)}) collective-permute-start(bf16[2,5,192,128]{3,2,1,0:T(8,128)(2,1)S(1)} %get-tuple-element.56), channel_id=1, source_target_pairs={{0,1},{1,0},{2,3},{3,2},{4,5},{5,4},{6,7},{7,6},{8,9},{9,8},{10,11... | collective-permute-start | bytes 1474568 | tf_op jit(solution)/shard_map/pair_out/ppermute | solution.py:258
  106.5 10.3 %collective-permute-start.12 = (bf16[2,2,384,128]{3,2,1,0:T(8,128)(2,1)S(1)}, bf16[2,2,384,128]{3,2,1,0:T(8,128)(2,1)S(1)}, u32[]{:S(2)}, u32[]{:S(2)}) collective-permute-start(bf16[2,2,384,128]{3,2,1,0:T(8,128)(2,1)S(1)} %get-tuple-element.62), channel_id=1, source_target_pairs={{0,2},{1,3},{2,0},{3,1},{4,6},{5,7},{6,4},{7,5},{8,10},{9,11},{10,... | collective-permute-start | bytes 1179656 | tf_op jit(solution)/shard_map/side_grads_0/ppermute | solution.py:258
  106.8 13.5 %collective-permute-start.18 = (bf16[2,2,384,128]{3,2,1,0:T(8,128)(2,1)S(1)}, bf16[2,2,384,128]{3,2,1,0:T(8,128)(2,1)S(1)}, u32[]{:S(2)}, u32[]{:S(2)}) collective-permute-start(bf16[2,2,384,128]{3,2,1,0:T(8,128)(2,1)S(1)} %pad_maximum_fusion.6), channel_id=1, source_target_pairs={{4,0},{5,1},{6,2},{7,3},{8,4},{9,5},{10,6},{11,7},{12,8},{13,9},{1... | collective-permute-start | bytes 1179656 | tf_op jit(solution)/shard_map/far_q_4/ppermute | solution.py:258
  114.6 10.6 %collective-permute-start.16 = (bf16[2,2,384,128]{3,2,1,0:T(8,128)(2,1)S(1)}, bf16[2,2,384,128]{3,2,1,0:T(8,128)(2,1)S(1)}, u32[]{:S(2)}, u32[]{:S(2)}) collective-permute-start(bf16[2,2,384,128]{3,2,1,0:T(8,128)(2,1)S(1)} %get-tuple-element.66), channel_id=1, source_target_pairs={{0,2},{1,3},{2,0},{3,1},{4,6},{5,7},{6,4},{7,5},{8,10},{9,11},{10,... | collective-permute-start | bytes 1179656 | tf_op jit(solution)/shard_map/side_grads_2/ppermute | solution.py:258
  116.8 14.2 %collective-permute-start.13 = (bf16[2,2,384,128]{3,2,1,0:T(8,128)(2,1)S(1)}, bf16[2,2,384,128]{3,2,1,0:T(8,128)(2,1)S(1)}, u32[]{:S(2)}, u32[]{:S(2)}) collective-permute-start(bf16[2,2,384,128]{3,2,1,0:T(8,128)(2,1)S(1)} %collective-permute-done.12.refs_2_), channel_id=1, source_target_pairs={{0,1},{1,0},{2,3},{3,2},{4,5},{5,4},{6,7},{7,6},{8,9},{9,8},{10,11... | collective-permute-start | bytes 1179656 | tf_op jit(solution)/shard_map/pair_of_grads_0/ppermute | solution.py:258
  123.6 6.6 %collective-permute-start.20 = (bf16[2,1,384,128]{3,2,1,0:T(8,128)(2,1)S(1)}, bf16[2,1,384,128]{3,2,1,0:T(8,128)(2,1)S(1)}, u32[]{:S(2)}, u32[]{:S(2)}) collective-permute-start(bf16[2,1,384,128]{3,2,1,0:T(8,128)(2,1)S(1)} %get-tuple-element.71), channel_id=1, source_target_pairs={{0,2},{1,3},{2,0},{3,1},{4,6},{5,7},{6,4},{7,5},{8,10},{9,11},{10,... | collective-permute-start | bytes 589832 | tf_op jit(solution)/shard_map/side_grads_4/ppermute | solution.py:258
  125.2 7.1 %collective-permute-start.17 = (bf16[2,2,384,128]{3,2,1,0:T(8,128)(2,1)S(1)}, bf16[2,2,384,128]{3,2,1,0:T(8,128)(2,1)S(1)}, u32[]{:S(2)}, u32[]{:S(2)}) collective-permute-start(bf16[2,2,384,128]{3,2,1,0:T(8,128)(2,1)S(1)} %collective-permute-done.16.refs_6_), channel_id=1, source_target_pairs={{0,1},{1,0},{2,3},{3,2},{4,5},{5,4},{6,7},{7,6},{8,9},{9,8},{10,11... | collective-permute-start | bytes 1179656 | tf_op jit(solution)/shard_map/pair_of_grads_2/ppermute | solution.py:258
  126.5 4.4 %collective-permute-start.11 = (bf16[2,2,192,128]{3,2,1,0:T(8,128)(2,1)S(1)}, bf16[2,2,192,128]{3,2,1,0:T(8,128)(2,1)S(1)}, u32[]{:S(2)}, u32[]{:S(2)}) collective-permute-start(bf16[2,2,192,128]{3,2,1,0:T(8,128)(2,1)S(1)} %get-tuple-element.61), channel_id=1, source_target_pairs={{0,1},{1,0},{2,3},{3,2},{4,5},{5,4},{6,7},{7,6},{8,9},{9,8},{10,11... | collective-permute-start | bytes 589832 | tf_op jit(solution)/shard_map/pair_grads_0/ppermute | solution.py:258
  126.5 4.5 %collective-permute-start.15 = (bf16[2,2,192,128]{3,2,1,0:T(8,128)(2,1)S(1)}, bf16[2,2,192,128]{3,2,1,0:T(8,128)(2,1)S(1)}, u32[]{:S(2)}, u32[]{:S(2)}) collective-permute-start(bf16[2,2,192,128]{3,2,1,0:T(8,128)(2,1)S(1)} %get-tuple-element.65), channel_id=1, source_target_pairs={{0,1},{1,0},{2,3},{3,2},{4,5},{5,4},{6,7},{7,6},{8,9},{9,8},{10,11... | collective-permute-start | bytes 589832 | tf_op jit(solution)/shard_map/pair_grads_2/ppermute | solution.py:258
  130.2 2.1 %collective-permute-start.21 = (bf16[2,1,384,128]{3,2,1,0:T(8,128)(2,1)S(1)}, bf16[2,1,384,128]{3,2,1,0:T(8,128)(2,1)S(1)}, u32[]{:S(2)}, u32[]{:S(2)}) collective-permute-start(bf16[2,1,384,128]{3,2,1,0:T(8,128)(2,1)S(1)} %collective-permute-done.20.refs_10_), channel_id=1, source_target_pairs={{0,1},{1,0},{2,3},{3,2},{4,5},{5,4},{6,7},{7,6},{8,9},{9,8},{10,11... | collective-permute-start | bytes 589832 | tf_op jit(solution)/shard_map/pair_of_grads_4/ppermute | solution.py:258
  131.0 1.3 collective-permute-start.19
